TPU v7x, 128 devices: a whole 4x4x4 slice. The times are simulated.
128 devices in a mesh: fsdp: 64 (over z, y_lo, x, core), tp: 2 (over y_hi).
Axes of the slice: x: 4, y: 4 (y_hi: 2, y_lo: 2; y = y_hi * 2 + y_lo), z: 4, core: 2. Of those that a mesh axis runs over, the one named last changes fastest.
Arguments:
- tokens: bfloat16 [8192, 4096], P('fsdp', 'tp'), may hold values from -6 to 6
- cotangent: bfloat16 [8192, 4096], P('fsdp', 'tp'), may hold values from -6 to 6
- routes: int32 [8192, 1], P('fsdp'), may hold values from 0 to 15; in each aligned block of 128 rows (0 to 127, 128 to 255, ...) at most 12 rows name the same one
- gates: float32 [8192, 1], P('fsdp'), may hold values from 0.02 to 0.25
- gate_proj: bfloat16 [64, 1024, 1536], P('fsdp', None, 'tp'), may hold values from -0.09375 to 0.09375
- up_proj: bfloat16 [64, 1024, 1536], P('fsdp', None, 'tp'), may hold values from -0.09375 to 0.09375
- down_proj: bfloat16 [64, 1536, 1024], P('fsdp', 'tp'), may hold values from -0.15625 to 0.15625
- gate_dir: bfloat16 [64, 1024, 1536], P('fsdp', None, 'tp'), may hold values from -0.09375 to 0.09375
- up_dir: bfloat16 [64, 1024, 1536], P('fsdp', None, 'tp'), may hold values from -0.09375 to 0.09375
- down_dir: bfloat16 [64, 1536, 1024], P('fsdp', 'tp'), may hold values from -0.15625 to 0.15625
Outputs:
- hvp_gate: float32 [64, 1024, 1536], P('fsdp', None, 'tp')
- hvp_up: float32 [64, 1024, 1536], P('fsdp', None, 'tp')
- hvp_down: float32 [64, 1536, 1024], P('fsdp', 'tp')
Inputs may be any that keep to these rules, and one draw needn't show every extreme that they name: `routes`: among the tokens of one device no expert is named more than 12 times.
All inputs are finite; a program needn't handle non-finite values.
Results may differ from a plain program's by a relative error of at most 0.0041.
Values may be sent and summed in bfloat16 or wider, within the bound.
A program may use at most 128 MiB of HBM per device.

v0:
```python
import jax
import jax.numpy as jnp
from jax import lax
from jax.sharding import PartitionSpec as P


def swapped(block, axis, apart):
    count = lax.axis_size(axis)
    route = []
    for low in range(count):
        high = low | 1 << apart
        if high != low and high < count:
            route += [(low, high), (high, low)]
    return lax.ppermute(block, axis, route)


def curvature(stacked, hidden_width):
    gate_pre = stacked[:, 0:hidden_width]
    up_pre = stacked[:, hidden_width : 2 * hidden_width]
    gate_tan = stacked[:, 2 * hidden_width : 3 * hidden_width]
    up_tan = stacked[:, 3 * hidden_width : 4 * hidden_width]
    grad_hidden = stacked[:, 4 * hidden_width : 5 * hidden_width]
    tan_grad = stacked[:, 5 * hidden_width : 6 * hidden_width]
    sigmoid_gate = jax.nn.sigmoid(gate_pre)
    silu_gate = gate_pre * sigmoid_gate
    slope = sigmoid_gate * (1.0 + gate_pre * (1.0 - sigmoid_gate))
    bend = sigmoid_gate * (1.0 - sigmoid_gate) * (2.0 + gate_pre * (1.0 - 2.0 * sigmoid_gate))
    tan_gate = (
        tan_grad * up_pre * slope
        + grad_hidden * up_tan * slope
        + grad_hidden * up_pre * bend * gate_tan
    )
    tan_up = tan_grad * silu_gate + grad_hidden * slope * gate_tan
    tan_hidden = slope * gate_tan * up_pre + silu_gate * up_tan
    return jnp.concatenate([tan_gate, tan_up, tan_hidden], axis=1).astype(jnp.bfloat16)


def local(
    tokens, cotangent, routes, gates, gate_proj, up_proj, down_proj, gate_dir, up_dir, down_dir
):
    full_tok, full_cot = (
        lax.all_gather(tokens, "tp", axis=1, tiled=True),
        lax.all_gather(cotangent, "tp", axis=1, tiled=True),
    )
    group_count = lax.axis_size("fsdp")
    expert_count = group_count // 4
    token_count = full_tok.shape[0]
    model_width = full_tok.shape[1]
    quarter_width = model_width // 4
    capacity = 3 * token_count // (2 * expert_count)
    route_list = routes.reshape(-1)
    per_token = routes.shape[1]
    pair_count = route_list.shape[0]
    onehot = (route_list[:, None] == jnp.arange(expert_count, dtype=jnp.int32)[None, :]).astype(
        jnp.int32
    )
    earlier = jnp.cumsum(onehot, axis=0) - onehot
    position_in = jnp.sum(earlier * onehot, axis=1)
    slot_table = (
        jnp.zeros((expert_count * capacity,), jnp.int32)
        .at[route_list * capacity + position_in]
        .set(jnp.arange(1, pair_count + 1, dtype=jnp.int32))
    )
    token_of = jnp.where(slot_table > 0, (slot_table - 1) // per_token + 1, 0)
    zero_row = jnp.zeros((1, model_width), jnp.bfloat16)
    send_tok = jnp.concatenate([zero_row, full_tok], axis=0)[token_of]
    row_weight = jnp.concatenate([jnp.zeros((1,), jnp.float32), gates.reshape(-1)])[slot_table]
    send_cot = (
        row_weight[:, None]
        * jnp.concatenate([zero_row, full_cot], axis=0)[token_of].astype(jnp.float32)
    ).astype(jnp.bfloat16)

    def arrange(rows):
        return (
            rows.reshape(expert_count, capacity, 4, quarter_width)
            .transpose(0, 2, 1, 3)
            .reshape(group_count * capacity, quarter_width)
        )

    local_tok, local_cot = (
        lax.all_to_all(arrange(send_tok), "fsdp", split_axis=0, concat_axis=0, tiled=True),
        lax.all_to_all(arrange(send_cot), "fsdp", split_axis=0, concat_axis=0, tiled=True),
    )
    hidden_width = gate_proj.shape[2]
    forward_weights = jnp.concatenate([gate_proj[0], up_proj[0], gate_dir[0], up_dir[0]], axis=1)
    backward_weights = jnp.concatenate([down_proj[0], down_dir[0]], axis=0)
    against = (((1,), (1,)), ((), ()))
    stacked = jnp.concatenate(
        [
            jnp.dot(local_tok, forward_weights, preferred_element_type=jnp.float32),
            lax.dot_general(
                local_cot, backward_weights, against, preferred_element_type=jnp.float32
            ),
        ],
        axis=1,
    )
    summed = stacked
    for bit_number in range(2):
        summed = summed + swapped(summed, "fsdp", bit_number)
    curved = curvature(summed, hidden_width)
    contract = (((0,), (0,)), ((), ()))
    hess_gate = lax.dot_general(
        local_tok, curved[:, 0:hidden_width], contract, preferred_element_type=jnp.float32
    )
    hess_up = lax.dot_general(
        local_tok,
        curved[:, hidden_width : 2 * hidden_width],
        contract,
        preferred_element_type=jnp.float32,
    )
    hess_down = lax.dot_general(
        curved[:, 2 * hidden_width : 3 * hidden_width],
        local_cot,
        contract,
        preferred_element_type=jnp.float32,
    )
    return (hess_gate[None], hess_up[None], hess_down[None])


def solution(mesh):
    return jax.shard_map(
        local,
        mesh=mesh,
        in_specs=(
            P("fsdp", "tp"),
            P("fsdp", "tp"),
            P("fsdp", None),
            P("fsdp", None),
            P("fsdp", None, "tp"),
            P("fsdp", None, "tp"),
            P("fsdp", "tp", None),
            P("fsdp", None, "tp"),
            P("fsdp", None, "tp"),
            P("fsdp", "tp", None),
        ),
        out_specs=(P("fsdp", None, "tp"), P("fsdp", None, "tp"), P("fsdp", "tp", None)),
        check_vma=False,
    )
```

profile of v0, /device:TPU:1, one launch (start us, length us, event | category | flops | bytes accessed | tf_op | source)
XLA Modules:
  0.0 514.7 jit_solution(13342247689740418707)
XLA Ops:
  7.2 0.0 all-gather.5.cloned.1.call-start
  7.2 0.7 all-gather.5.cloned.1.call-update
  7.9 0.7 fusion.25
  8.6 0.2 reduce_window_sum.11
  8.8 0.8 select_reduce_fusion
  9.6 0.7 fusion.26
  10.3 1.0 scatter_custom_fusion
  11.3 0.7 pad_maximum_fusion.1
  12.0 1.6 gather_fusion.1
  13.7 0.1 mul.84
  13.7 0.1 copy.24
  13.8 24.4 %all-gather.5.cloned.1.call-done = bf16[128,4096]{1,0:T(8,128)(2,1)} async-done(((bf16[128,2048]{1,0:T(8,128)(2,1)}), bf16[128,4096]{1,0:T(8,128)(2,1)}) %all-gather.5.cloned.1.call-update) | async-done | bytes 1048592 | tf_op jit(solution)/shard_map/all_gather | solution.py:43
  38.3 1.5 concatenate.23
  39.8 2.7 gather_fusion.2
  42.4 3.8 reshape.34
  46.2 0.6 fusion.21
  46.8 2.2 copy.28
  49.0 8.1 %all-to-all-start.1 = ((bf16[64,12,1024]{2,1,0:T(8,128)(2,1)}), bf16[64,12,1024]{2,1,0:T(8,128)(2,1)S(1)}, u32[]{:S(2)}, u32[]{:S(2)}) async-start(bf16[64,12,1024]{2,1,0:T(8,128)(2,1)} %bitcast.34), calls=%async_computation.1 | async-start | bytes 4194304 | tf_op jit(solution)/shard_map/all_to_all | solution.py:82
  57.1 0.0 all-gather.3.cloned.1.call-start
  57.2 0.7 all-gather.3.cloned.1.call-update
  57.9 36.6 %all-gather.3.cloned.1.call-done = bf16[128,4096]{1,0:T(8,128)(2,1)} async-done(((bf16[128,2048]{1,0:T(8,128)(2,1)}), bf16[128,4096]{1,0:T(8,128)(2,1)}) %all-gather.3.cloned.1.call-update) | async-done | bytes 1048592 | tf_op jit(solution)/shard_map/all_gather | solution.py:42
  94.5 1.5 concatenate.20
  96.0 2.7 gather_fusion
  98.7 3.9 reshape.32
  102.6 3.4 copy.27
  106.0 0.0 all-to-all-done.1
  106.0 9.1 %all-to-all-start = ((bf16[64,12,1024]{2,1,0:T(8,128)(2,1)}), bf16[64,12,1024]{2,1,0:T(8,128)(2,1)}, u32[]{:S(2)}, u32[]{:S(2)}) async-start(bf16[64,12,1024]{2,1,0:T(8,128)(2,1)} %bitcast.35), calls=%async_computation | async-start | bytes 4194304 | tf_op jit(solution)/shard_map/all_to_all | solution.py:81
  115.0 1.3 all_to_all.21
  116.4 7.1 %fusion.8 = f32[768,1536]{1,0:T(8,128)} fusion(bf16[768,1024]{1,0:T(8,128)(2,1)} %all_to_all.21, bf16[768,1024]{1,0:T(8,128)(2,1)} %bitcast.40, bf16[768,1024]{1,0:T(8,128)(2,1)} %bitcast.41), kind=kOutput, calls=%fused_computation.15 | convolution fusion | flops 2422210560 | bytes 9437184 | tf_op jit(solution)/shard_map/dot_general | solution.py:91
  123.5 20.8 %all-to-all-done = bf16[64,12,1024]{2,1,0:T(8,128)(2,1)} async-done(((bf16[64,12,1024]{2,1,0:T(8,128)(2,1)}), bf16[64,12,1024]{2,1,0:T(8,128)(2,1)}, u32[]{:S(2)}, u32[]{:S(2)}) %all-to-all-start) | async-done | bytes 1572896 | tf_op jit(solution)/shard_map/all_to_all | solution.py:81
  144.3 0.0 slice-start
  144.3 2.6 all_to_all.18
  146.9 0.0 slice-start.1
  146.9 7.8 %fusion = f32[768,3072]{1,0:T(8,128)S(1)} fusion(bf16[768,1024]{1,0:T(8,128)(2,1)S(1)} %all_to_all.18, bf16[1024,768]{1,0:T(8,128)(2,1)} %bitcast.42, bf16[1024,768]{1,0:T(8,128)(2,1)} %bitcast.43, bf16[1024,768]{1,0:T(8,128)(2,1)} %bitcast.44, bf16[1024,768]{1,0:T(8,128)(2,1)} %bitcast.45), kind=kOutput, calls=%fused_computation.5 | convolution fusion | flops 4857004032 | bytes 17301504 | tf_op jit(solution)/shard_map/dot_general | solution.py:90
  154.7 0.0 slice-done
  154.7 0.0 slice-done.1
  154.7 1.2 pad_maximum_fusion
  155.9 0.1 collective-permute-start
  156.0 21.5 %collective-permute-done = f32[768,4608]{1,0:T(8,128)} collective-permute-done((f32[768,4608]{1,0:T(8,128)S(1)}, f32[768,4608]{1,0:T(8,128)}, u32[]{:S(2)}, u32[]{:S(2)}) %collective-permute-start) | collective-permute-done | bytes 14155808 | tf_op jit(solution)/shard_map/ppermute | solution.py:14
  177.5 6.3 %fusion.35 = f32[768,4608]{1,0:T(8,128)S(1)} fusion(f32[768,4608]{1,0:T(8,128)} %collective-permute-done, f32[768,1536]{1,0:T(8,128)S(1)} %bitcast.33, f32[768,3072]{1,0:T(8,128)S(1)} %fusion), kind=kLoop, calls=%fused_computation.57 | loop fusion | flops 7077888 | bytes 42467328 | tf_op jit(solution)/shard_map/add | solution.py:99
  183.9 0.0 copy-start
  183.9 0.7 collective-permute-start.1
  184.6 305.2 %collective-permute-done.1 = f32[768,4608]{1,0:T(8,128)} collective-permute-done((f32[768,4608]{1,0:T(8,128)S(1)}, f32[768,4608]{1,0:T(8,128)}, u32[]{:S(2)}, u32[]{:S(2)}) %collective-permute-start.1) | collective-permute-done | bytes 14155808 | tf_op jit(solution)/shard_map/ppermute | solution.py:14
  489.8 6.3 %add.70 = f32[768,4608]{1,0:T(8,128)S(1)} add(f32[768,4608]{1,0:T(8,128)S(1)} %fusion.35, f32[768,4608]{1,0:T(8,128)} %collective-permute-done.1) | non-fusion elementwise | flops 3538944 | bytes 42467328 | tf_op jit(solution)/shard_map/add | solution.py:99
  496.1 0.0 copy-done
  496.1 3.9 convolution_bitcast_fusion
  500.0 3.6 convolution_bitcast_fusion.1
  503.7 4.2 convolution_bitcast_fusion.2
  (5 shorter events, 0.0 us)
Async XLA Ops:
  7.2 31.1 %all-gather.5.cloned.1.call-start = ((), (), s32[]{:S(2)}) async-start(), calls=%async_computation.3 | async-start | bytes 1572864 | tf_op jit(solution)/shard_map/all_gather | solution.py:43
  49.0 56.9 %all-to-all-start.1 = ((bf16[64,12,1024]{2,1,0:T(8,128)(2,1)}), bf16[64,12,1024]{2,1,0:T(8,128)(2,1)S(1)}, u32[]{:S(2)}, u32[]{:S(2)}) async-start(bf16[64,12,1024]{2,1,0:T(8,128)(2,1)} %bitcast.34), calls=%async_computation.1 | async-start | bytes 4194304 | tf_op jit(solution)/shard_map/all_to_all | solution.py:82
  57.1 37.4 %all-gather.3.cloned.1.call-start = ((), (), s32[]{:S(2)}) async-start(), calls=%async_computation.2 | async-start | bytes 1572864 | tf_op jit(solution)/shard_map/all_gather | solution.py:42
  106.0 38.3 %all-to-all-start = ((bf16[64,12,1024]{2,1,0:T(8,128)(2,1)}), bf16[64,12,1024]{2,1,0:T(8,128)(2,1)}, u32[]{:S(2)}, u32[]{:S(2)}) async-start(bf16[64,12,1024]{2,1,0:T(8,128)(2,1)} %bitcast.35), calls=%async_computation | async-start | bytes 4194304 | tf_op jit(solution)/shard_map/all_to_all | solution.py:81
  144.3 10.4 %slice-start = ((s8[4718592]{0:T(1024)(128)(4,1)}), s8[524288]{0:T(1024)(128)(4,1)S(1)}, s32[]{:S(2)}) async-start(s8[4718592]{0:T(1024)(128)(4,1)} %bitcast.32), calls=%async_computation.4 | async-start | bytes 1048576
  146.9 7.8 %slice-start.1 = ((s8[4718592]{0:T(1024)(128)(4,1)}), s8[4194304]{0:T(1024)(128)(4,1)S(1)}, s32[]{:S(2)}) async-start(s8[4718592]{0:T(1024)(128)(4,1)} %bitcast.32), calls=%async_computation.5 | async-start | bytes 8388608
  155.9 21.6 %collective-permute-start = (f32[768,4608]{1,0:T(8,128)S(1)}, f32[768,4608]{1,0:T(8,128)}, u32[]{:S(2)}, u32[]{:S(2)}) collective-permute-start(f32[768,4608]{1,0:T(8,128)S(1)} %pad_maximum_fusion), channel_id=1, source_target_pairs={{0,2},{2,0},{4,6},{6,4},{8,10},{10,8},{12,14},{14,12},{16,18},{18,... | collective-permute-start | bytes 42467336 | tf_op jit(solution)/shard_map/ppermute | solution.py:14
  183.9 312.3 %copy-start = (bf16[768,1024]{1,0:T(8,128)(2,1)S(1)}, bf16[768,1024]{1,0:T(8,128)(2,1)}, u32[]{:S(2)}) copy-start(bf16[768,1024]{1,0:T(8,128)(2,1)} %all_to_all.21) | copy-start | bytes 4718596
  183.9 305.9 %collective-permute-start.1 = (f32[768,4608]{1,0:T(8,128)S(1)}, f32[768,4608]{1,0:T(8,128)}, u32[]{:S(2)}, u32[]{:S(2)}) collective-permute-start(f32[768,4608]{1,0:T(8,128)S(1)} %fusion.35), channel_id=1, source_target_pairs={{0,4},{4,0},{2,6},{6,2},{8,12},{12,8},{10,14},{14,10},{16,20},{20,... | collective-permute-start | bytes 42467336 | tf_op jit(solution)/shard_map/ppermute | solution.py:14
Sparse Core Ops, SparseCore 0:
  9.7 28.5 all-gather.4
  59.6 34.8 all-gather.2
where the time goes:
time: 515 us
  waiting for transfers between devices  410 us (80%)
  local copies, waits for them, and re-layouts  28.2 us (5%)
  matrix products  26.7 us (5%)
  starting transfers between devices  18 us (3%)
  other arithmetic  17.6 us (3%)
  between operations  14.2 us (3%)
    ppermute x2, waiting for transfers between devices, swapped(): return lax.ppermute(block, axis, route)  327 us
    all_gather x1, waiting for transfers between devices, local(): lax.all_gather(tokens, 'tp', axis=1, tiled=True)  36.6 us
    all_gather x1, waiting for transfers between devices, local(): lax.all_gather(cotangent, 'tp', axis=1, tiled=True)  24.4 us
    all_to_all x1, waiting for transfers between devices, local(): lax.all_to_all(arrange(send_tok), 'fsdp', split_axis=0, concat_axis=0, ti...  20.8 us
    add x2, other arithmetic, local(): summed = summed + swapped(summed, 'fsdp', bit_number)  12.7 us
  transfers between devices with their start and end apart: 6, of which 5 were waited for; matrix products, arithmetic and copies ran while one was open for 5% of the time, Pallas kernels for 0%

commit v1 on v0

v1 whole, which is shorter than its diff:
```python
import jax
import jax.numpy as jnp
from jax import lax
from jax.experimental import pallas as pl
from jax.experimental.pallas import tpu as pltpu
from jax.sharding import PartitionSpec as P

MESH = pl.DeviceIdType.MESH
CAPACITY = 12
BLOCK = 4 * CAPACITY
VMEM_LIMIT = 60 * 1024 * 1024
SPACE = pl.BlockSpec(memory_space=pltpu.VMEM)
HBM = pl.BlockSpec(memory_space=pl.ANY)


def dispatch_kernel(
    tok_ref, cot_ref, row_ref, col_ref, gate_ref, out_ref, send_ref, pick_ref, feed_ref, send_sem, recv_sem
):
    tokens, width = tok_ref.shape
    fine = width // 4
    groups = out_ref.shape[0] // BLOCK
    experts = groups // 4
    me, half = lax.axis_index("fsdp"), lax.axis_index("tp")
    source_half = (me % 4) // 2
    keeps_own = source_half == half

    barrier = pltpu.get_barrier_semaphore()

    def greet(other, carry):
        @pl.when(jnp.logical_or(other != me, source_half != half))
        def _():
            pl.semaphore_signal(barrier, inc=1, device_id=(other, source_half), device_id_type=MESH)

        return carry

    lax.fori_loop(0, groups, greet, 0)

    row, col = row_ref[...], col_ref[...]
    first = lax.broadcasted_iota(jnp.int32, (tokens, tokens), 0)
    second = lax.broadcasted_iota(jnp.int32, (tokens, tokens), 1)
    before = jnp.where((col == row) & (first < second), 1.0, 0.0)
    slot = row.astype(jnp.float32) * CAPACITY + jnp.sum(before, axis=0, keepdims=True)
    key = jnp.concatenate([slot + 1024.0 * part for part in range(4)], axis=1)
    place = lax.broadcasted_iota(jnp.int32, (experts * BLOCK, 1), 0).astype(jnp.float32)
    expert = jnp.floor((place + 0.5) * (1.0 / BLOCK))
    within = place - expert * BLOCK
    part = jnp.floor((within + 0.5) * (1.0 / CAPACITY))
    wanted = expert * CAPACITY + (within - part * CAPACITY) + 1024.0 * part
    pick_ref[...] = jnp.where(wanted == key, 1.0, 0.0).astype(jnp.bfloat16)
    weighted = (gate_ref[...] * cot_ref[...].astype(jnp.float32)).astype(jnp.bfloat16)
    for piece in range(2):
        for side in range(2):
            lanes = slice((2 * piece + side) * fine, (2 * piece + side + 1) * fine)
            feed_ref[piece, pl.ds(side * tokens, tokens), :] = tok_ref[:, lanes]
            feed_ref[piece, pl.ds((2 + side) * tokens, tokens), :] = weighted[:, lanes]

    pl.semaphore_wait(barrier, groups - jnp.where(keeps_own, 1, 0))

    def remote(expert, piece, side, number):
        target = 4 * expert + 2 * half + piece
        return pltpu.make_async_remote_copy(
            src_ref=send_ref.at[piece, pl.ds(pl.multiple_of(expert * BLOCK, BLOCK), BLOCK), :],
            dst_ref=out_ref.at[pl.ds(pl.multiple_of(me * BLOCK, BLOCK), BLOCK), :],
            send_sem=send_sem.at[number],
            recv_sem=recv_sem.at[me],
            device_id=(target, side),
            device_id_type=MESH,
        )

    def numbered(step):
        expert = (me // 4 + step) % experts
        return expert

    def send(step, carry):
        expert = numbered(step)
        base = pl.multiple_of(expert * BLOCK, BLOCK)
        for piece in range(2):
            send_ref[piece, pl.ds(base, BLOCK), :] = jnp.dot(
                pick_ref[pl.ds(base, BLOCK), :], feed_ref[piece], preferred_element_type=jnp.float32
            ).astype(jnp.bfloat16)
            for side in range(2):
                target = 4 * expert + 2 * half + piece
                here = jnp.logical_and(target == me, half == side)
                number = step * 4 + piece * 2 + side

                @pl.when(jnp.logical_not(here))
                def _():
                    remote(expert, piece, side, number).start()

                @pl.when(here)
                def _():
                    pltpu.make_async_copy(
                        send_ref.at[piece, pl.ds(base, BLOCK), :],
                        out_ref.at[pl.ds(pl.multiple_of(me * BLOCK, BLOCK), BLOCK), :],
                        recv_sem.at[me],
                    ).start()

        return carry

    lax.fori_loop(0, experts, send, 0)

    def drain(source, carry):
        block = out_ref.at[pl.ds(pl.multiple_of(source * BLOCK, BLOCK), BLOCK), :]
        pltpu.make_async_copy(block, block, recv_sem.at[source]).wait()
        return carry

    lax.fori_loop(0, groups, drain, 0)

    def sent(step, carry):
        expert = numbered(step)
        for piece in range(2):
            for side in range(2):
                target = 4 * expert + 2 * half + piece

                @pl.when(jnp.logical_not(jnp.logical_and(target == me, half == side)))
                def _():
                    remote(expert, piece, side, step * 4 + piece * 2 + side).wait_send()

        return carry

    lax.fori_loop(0, experts, sent, 0)


def curvature(total, width):
    gate_pre, up_pre, gate_tan, up_tan, grad_hidden, tan_grad = (
        total[:, width * place : width * (place + 1)] for place in range(6)
    )
    sigmoid_gate = jax.nn.sigmoid(gate_pre)
    silu_gate = gate_pre * sigmoid_gate
    slope = sigmoid_gate * (1.0 + gate_pre * (1.0 - sigmoid_gate))
    bend = sigmoid_gate * (1.0 - sigmoid_gate) * (2.0 + gate_pre * (1.0 - 2.0 * sigmoid_gate))
    tan_gate = (
        tan_grad * up_pre * slope
        + grad_hidden * up_tan * slope
        + grad_hidden * up_pre * bend * gate_tan
    )
    tan_up = tan_grad * silu_gate + grad_hidden * slope * gate_tan
    tan_hidden = slope * gate_tan * up_pre + silu_gate * up_tan
    return jnp.concatenate([tan_gate, tan_up, tan_hidden], axis=1).astype(jnp.bfloat16)


def group_kernel(
    packed_ref, gate_ref, up_ref, gdir_ref, udir_ref, down_ref, ddir_ref,
    tok_ref, cot_ref, curved_ref,
    fwd_ref, bwd_ref, keep_ref, core_out, core_in, chip_keep, chip_out, chip_in,
    load_sem, core_send, core_recv, chip_send, chip_recv, back_send, back_recv, last_send, last_recv,
):
    rows, depth = tok_ref.shape
    chunks, _, wide = curved_ref.shape
    slim = wide // 3
    halved, quarter = rows // 2, rows // 4
    me, side = lax.axis_index("fsdp"), lax.axis_index("tp")
    core, chip = me % 2, (me % 4) // 2
    core_mate = (me + 1 - 2 * core, side)
    chip_mate = (me + 2 - 4 * chip, side)

    def loads(chunk):
        at = slice(chunk * slim, (chunk + 1) * slim)
        pieces = [
            (ref.at[:, at], fwd_ref.at[chunk, :, pl.ds(place * slim, slim)])
            for place, ref in enumerate((gate_ref, up_ref, gdir_ref, udir_ref))
        ] + [
            (ref.at[at, :], bwd_ref.at[chunk, pl.ds(place * slim, slim), :])
            for place, ref in enumerate((down_ref, ddir_ref))
        ]
        return [
            pltpu.make_async_copy(source, target, load_sem.at[chunk, place])
            for place, (source, target) in enumerate(pieces)
        ]

    barrier = pltpu.get_barrier_semaphore()
    for mate in (core_mate, chip_mate):
        pl.semaphore_signal(barrier, inc=1, device_id=mate, device_id_type=MESH)
    for chunk in range(chunks):
        for copy in loads(chunk):
            copy.start()

    sort_rows = 4 * BLOCK
    left = lax.broadcasted_iota(jnp.int32, (sort_rows, 1), 0).astype(jnp.float32)
    source = jnp.floor((left + 0.5) * (1.0 / BLOCK))
    part = jnp.floor((left - source * BLOCK + 0.5) * (1.0 / CAPACITY))
    rest = left - source * BLOCK - part * CAPACITY
    out_part, out_source, out_rest = source, part, rest
    wanted = out_source * BLOCK + out_part * CAPACITY + out_rest
    have = lax.broadcasted_iota(jnp.int32, (1, sort_rows), 1).astype(jnp.float32)
    sorter = jnp.where(wanted == have, 1.0, 0.0).astype(jnp.bfloat16)
    fine = depth // 2

    def sort(group, carry):
        block = packed_ref[pl.ds(pl.multiple_of(group * sort_rows, sort_rows), sort_rows), :]
        ordered = jnp.dot(sorter, block, preferred_element_type=jnp.float32).astype(jnp.bfloat16)
        to = pl.ds(pl.multiple_of(group * BLOCK, BLOCK), BLOCK)
        tok_ref[to, 0:fine] = ordered[0:BLOCK]
        tok_ref[to, fine:depth] = ordered[BLOCK : 2 * BLOCK]
        cot_ref[to, 0:fine] = ordered[2 * BLOCK : 3 * BLOCK]
        cot_ref[to, fine:depth] = ordered[3 * BLOCK : 4 * BLOCK]
        return carry

    lax.fori_loop(0, rows // BLOCK, sort, 0)
    pl.semaphore_wait(barrier, 2)

    against = (((1,), (1,)), ((), ()))

    def to_core(chunk):
        return pltpu.make_async_remote_copy(
            src_ref=core_out.at[chunk], dst_ref=core_in.at[chunk],
            send_sem=core_send.at[chunk], recv_sem=core_recv.at[chunk],
            device_id=core_mate, device_id_type=MESH,
        )

    def to_chip(chunk):
        return pltpu.make_async_remote_copy(
            src_ref=chip_out.at[chunk], dst_ref=chip_in.at[chunk],
            send_sem=chip_send.at[chunk], recv_sem=chip_recv.at[chunk],
            device_id=chip_mate, device_id_type=MESH,
        )

    def back(chunk, where):
        place = curved_ref.at[chunk, pl.ds(pl.multiple_of(where, quarter), quarter), :]
        return pltpu.make_async_remote_copy(
            src_ref=place, dst_ref=place,
            send_sem=back_send.at[chunk], recv_sem=back_recv.at[chunk],
            device_id=chip_mate, device_id_type=MESH,
        )

    def last(chunk, where):
        place = curved_ref.at[chunk, pl.ds(pl.multiple_of(where, halved), halved), :]
        return pltpu.make_async_remote_copy(
            src_ref=place, dst_ref=place,
            send_sem=last_send.at[chunk], recv_sem=last_recv.at[chunk],
            device_id=core_mate, device_id_type=MESH,
        )

    my_half, mate_half = core * halved, (1 - core) * halved
    my_quarter = my_half + chip * quarter
    mate_quarter = my_half + (1 - chip) * quarter

    def forward(chunk, begin, into):
        at = pl.ds(pl.multiple_of(begin, halved), halved)
        into[chunk, :, 0 : 4 * slim] = jnp.dot(
            tok_ref[at, :], fwd_ref[chunk], preferred_element_type=jnp.float32
        )
        into[chunk, :, 4 * slim : 6 * slim] = lax.dot_general(
            cot_ref[at, :], bwd_ref[chunk], against, preferred_element_type=jnp.float32
        )

    def products(chunk):
        for place in range(6):
            pltpu.make_async_copy(
                bwd_ref.at[chunk, pl.ds(0, slim), :] if place >= 4 else fwd_ref.at[chunk, :, pl.ds(0, slim)],
                bwd_ref.at[chunk, pl.ds(0, slim), :] if place >= 4 else fwd_ref.at[chunk, :, pl.ds(0, slim)],
                load_sem.at[chunk, place],
            ).wait()
        forward(chunk, mate_half, core_out)
        to_core(chunk).start()
        forward(chunk, my_half, keep_ref)

    def core_sum(chunk):
        to_core(chunk).wait_recv()
        theirs = pl.ds(pl.multiple_of((1 - chip) * quarter, quarter), quarter)
        chip_out[chunk] = (keep_ref[chunk, theirs, :] + core_in[chunk, theirs, :]).astype(jnp.bfloat16)
        to_chip(chunk).start()
        ours = pl.ds(pl.multiple_of(chip * quarter, quarter), quarter)
        chip_keep[chunk] = keep_ref[chunk, ours, :] + core_in[chunk, ours, :]

    def first_pass(step, carry):
        @pl.when(step < chunks)
        def _():
            products(step)

        @pl.when(step > 0)
        def _():
            core_sum(step - 1)

        return carry

    lax.fori_loop(0, chunks + 1, first_pass, 0)

    def curve(chunk, carry):
        to_chip(chunk).wait_recv()
        total = chip_keep[chunk] + chip_in[chunk].astype(jnp.float32)
        curved_ref[chunk, pl.ds(pl.multiple_of(my_quarter, quarter), quarter), :] = curvature(total, slim)
        back(chunk, my_quarter).start()
        return carry

    lax.fori_loop(0, chunks, curve, 0)

    def spread(chunk, carry):
        back(chunk, mate_quarter).wait_recv()
        last(chunk, my_half).start()
        return carry

    lax.fori_loop(0, chunks, spread, 0)

    def finish(chunk, carry):
        last(chunk, mate_half).wait_recv()
        to_core(chunk).wait_send()
        to_chip(chunk).wait_send()
        back(chunk, my_quarter).wait_send()
        last(chunk, my_half).wait_send()
        return carry

    lax.fori_loop(0, chunks, finish, 0)


def product_kernel(tok_ref, cot_ref, curved_ref, gate_out, up_out, down_out, flipped):
    slim = curved_ref.shape[2] // 3

    @pl.when(pl.program_id(0) == 0)
    def _():
        flipped[...] = tok_ref[...].T

    both = jnp.dot(flipped[...], curved_ref[0, :, 0 : 2 * slim], preferred_element_type=jnp.float32)
    gate_out[...] = both[:, 0:slim]
    up_out[...] = both[:, slim : 2 * slim]
    down_out[...] = lax.dot_general(
        curved_ref[0, :, 2 * slim : 3 * slim],
        cot_ref[...],
        (((0,), (0,)), ((), ())),
        preferred_element_type=jnp.float32,
    )


def local(
    tokens, cotangent, routes, gates, gate_proj, up_proj, down_proj, gate_dir, up_dir, down_dir
):
    count, width = tokens.shape
    groups = lax.axis_size("fsdp")
    experts = groups // 4
    depth, hidden = gate_proj.shape[1:]
    rows = groups * CAPACITY
    slim = 128
    chunks = hidden // slim
    halved, quarter = rows // 2, rows // 4
    bf16, f32 = jnp.bfloat16, jnp.float32

    packed = pl.pallas_call(
        dispatch_kernel,
        name="dispatch",
        out_shape=jax.ShapeDtypeStruct((groups * BLOCK, width // 4), bf16),
        in_specs=[SPACE] * 5,
        out_specs=HBM,
        scratch_shapes=[
            pltpu.VMEM((2, experts * BLOCK, width // 4), bf16),
            pltpu.VMEM((experts * BLOCK, 4 * count), bf16),
            pltpu.VMEM((2, 4 * count, width // 4), bf16),
            pltpu.SemaphoreType.DMA((groups,)),
            pltpu.SemaphoreType.DMA((groups,)),
        ],
        compiler_params=pltpu.CompilerParams(
            collective_id=0, has_side_effects=True, vmem_limit_bytes=VMEM_LIMIT
        ),
    )(tokens, cotangent, routes.reshape(1, count), routes, gates)

    tok, cot, curved = pl.pallas_call(
        group_kernel,
        name="group",
        out_shape=(
            jax.ShapeDtypeStruct((rows, depth), bf16),
            jax.ShapeDtypeStruct((rows, depth), bf16),
            jax.ShapeDtypeStruct((chunks, rows, 3 * slim), bf16),
        ),
        in_specs=[SPACE] + [HBM] * 6,
        out_specs=(SPACE,) * 3,
        scratch_shapes=[
            pltpu.VMEM((chunks, depth, 4 * slim), bf16),
            pltpu.VMEM((chunks, 2 * slim, depth), bf16),
            pltpu.VMEM((chunks, halved, 6 * slim), f32),
            pltpu.VMEM((chunks, halved, 6 * slim), f32),
            pltpu.VMEM((chunks, halved, 6 * slim), f32),
            pltpu.VMEM((chunks, quarter, 6 * slim), f32),
            pltpu.VMEM((chunks, quarter, 6 * slim), bf16),
            pltpu.VMEM((chunks, quarter, 6 * slim), bf16),
            pltpu.SemaphoreType.DMA((chunks, 6)),
        ]
        + [pltpu.SemaphoreType.DMA((chunks,))] * 8,
        compiler_params=pltpu.CompilerParams(
            collective_id=1, has_side_effects=True, vmem_limit_bytes=VMEM_LIMIT
        ),
    )(packed, gate_proj[0], up_proj[0], gate_dir[0], up_dir[0], down_proj[0], down_dir[0])

    whole = lambda chunk: (0, 0)
    hess_gate, hess_up, hess_down = pl.pallas_call(
        product_kernel,
        name="products",
        grid=(chunks,),
        out_shape=(
            jax.ShapeDtypeStruct((depth, hidden), f32),
            jax.ShapeDtypeStruct((depth, hidden), f32),
            jax.ShapeDtypeStruct((hidden, depth), f32),
        ),
        in_specs=[
            pl.BlockSpec((rows, depth), whole),
            pl.BlockSpec((rows, depth), whole),
            pl.BlockSpec((1, rows, 3 * slim), lambda chunk: (chunk, 0, 0)),
        ],
        out_specs=(
            pl.BlockSpec((depth, slim), lambda chunk: (0, chunk)),
            pl.BlockSpec((depth, slim), lambda chunk: (0, chunk)),
            pl.BlockSpec((slim, depth), lambda chunk: (chunk, 0)),
        ),
        scratch_shapes=[pltpu.VMEM((depth, rows), bf16)],
        compiler_params=pltpu.CompilerParams(vmem_limit_bytes=VMEM_LIMIT),
    )(tok, cot, curved)
    return (hess_gate[None], hess_up[None], hess_down[None])


def solution(mesh):
    return jax.shard_map(
        local,
        mesh=mesh,
        in_specs=(
            P("fsdp", "tp"),
            P("fsdp", "tp"),
            P("fsdp", None),
            P("fsdp", None),
            P("fsdp", None, "tp"),
            P("fsdp", None, "tp"),
            P("fsdp", "tp", None),
            P("fsdp", None, "tp"),
            P("fsdp", None, "tp"),
            P("fsdp", "tp", None),
        ),
        out_specs=(P("fsdp", None, "tp"), P("fsdp", None, "tp"), P("fsdp", "tp", None)),
        check_vma=False,
    )
```

time: 515 us -> 169 us (0.33)
  waiting for transfers between devices: 410 us -> 0 us
  Pallas kernels: 0 us -> 166 us
  matrix products: 26.7 us -> 0 us
  local copies, waits for them, and re-layouts: 28.2 us -> 2.78 us
  starting transfers between devices: 18 us -> 0 us
  other arithmetic: 17.6 us -> 0 us
  between operations: 14.2 us -> 0.65 us
    ppermute x2 -> x0, waiting for transfers between devices: 327 us -> none  [swapped(): return lax.ppermute(block, axis, route)]
    pallas_call x0 -> x3, Pallas kernels: none -> 166 us  [the longest x1 81.6 us: local(): pl.pallas_call(dispatch_kernel, name='dispatch', out_shape=jax.ShapeDtype...]
    all_gather x2 -> x0, waiting for transfers between devices: 61.1 us -> none  [the longest x1 36.6 us: local(): lax.all_gather(tokens, 'tp', axis=1, tiled=True)]
    dot_general x5 -> x0, matrix products: 26.7 us -> none  [the longest x1 7.79 us: local(): jnp.dot(local_tok, forward_weights, preferred_element_type=jnp.float32)]
    all_to_all x2 -> x0, waiting for transfers between devices: 20.8 us -> none  [the longest x1 20.8 us: local(): lax.all_to_all(arrange(send_tok), 'fsdp', split_axis=0, concat_axis=0, ti...]
    all_to_all x2 -> x0, starting transfers between devices: 17.2 us -> none  [the longest x1 9.06 us: local(): lax.all_to_all(arrange(send_tok), 'fsdp', split_axis=0, concat_axis=0, ti...]
    add x3 -> x0, other arithmetic: 12.7 us -> none  [the longest x2 12.7 us: local(): summed = summed + swapped(summed, 'fsdp', bit_number)]
    all_to_all x4 -> x0, local copies, waits for them, and re-layouts: 9.49 us -> none  [the longest x2 5.95 us: local(): lax.all_to_all(arrange(send_tok), 'fsdp', split_axis=0, concat_axis=0, ti...]
  transfers between devices with their start and end apart: 6 -> 0, of which waited for: 5 -> 0; matrix products, arithmetic and copies ran while one was open for 5% -> 0% of each run, Pallas kernels for 0% -> 0%
where the time goes in v1:
time: 169 us
  Pallas kernels  166 us (98%)
  local copies, waits for them, and re-layouts  2.78 us (2%)
    pallas_call x1, Pallas kernels, local(): pl.pallas_call(dispatch_kernel, name='dispatch', out_shape=jax.ShapeDtype...  81.6 us
    pallas_call x1, Pallas kernels, local(): pl.pallas_call(group_kernel, name='group', out_shape=(jax.ShapeDtypeStruc...  73.9 us
    pallas_call x1, Pallas kernels, local(): pl.pallas_call(product_kernel, name='products', grid=(chunks,), out_shape...  10.2 us

profile of v1, /device:TPU:1, one launch (start us, length us, event | category | flops | bytes accessed | tf_op | source)
XLA Modules:
  0.0 169.2 jit_solution(1676965905033923299)
XLA Ops:
  0.6 1.4 copy.14.gate_ref
  2.0 1.4 copy.13.col_ref
  3.4 81.6 %dispatch.1.packed_ref = bf16[3072,512]{1,0:T(8,128)(2,1)} custom-call(bf16[128,2048]{1,0:T(8,128)(2,1)} %tok_ref.1, bf16[128,2048]{1,0:T(8,128)(2,1)} %cot_ref.1, s32[1,128]{1,0:T(1,128)} %bitcast.16, s32[128,1]{1,0:T(8,128)} %copy.13.col_ref, f32[128,1]{1,0:T(8,128)} %copy.14.gate_ref), custom_call_target="tpu_custom_call" | custom-call | tf_op jit(solution)/shard_map/dispatch/pallas_call | solution.py:337
  85.0 73.9 %group.1 = (bf16[768,1024]{1,0:T(8,128)(2,1)}, bf16[768,1024]{1,0:T(8,128)(2,1)}, bf16[6,768,384]{2,1,0:T(8,128)(2,1)}) custom-call(bf16[3072,512]{1,0:T(8,128)(2,1)} %dispatch.1.packed_ref, bf16[1024,768]{1,0:T(8,128)(2,1)} %bitcast.10, bf16[1024,768]{1,0:T(8,128)(2,1)} %bitcast.11, bf16[1024,768]{1,0:T(8,128)(2,1)} %bitcast.12, ...), custom_call_target="tpu_custom_call" | custom-call | tf_op jit(solution)/shard_map/group/pallas_call | solution.py:355
  159.0 10.2 %products.1 = (f32[1024,768]{1,0:T(8,128)}, f32[1024,768]{1,0:T(8,128)}, f32[768,1024]{1,0:T(8,128)}) custom-call(bf16[768,1024]{1,0:T(8,128)(2,1)} %get-tuple-element.9.tok_ref, bf16[768,1024]{1,0:T(8,128)(2,1)} %get-tuple-element.10.cot_ref, bf16[6,768,384]{2,1,0:T(8,128)(2,1)} %get-tuple-element.11.curved_ref), custom_call_target="tpu_custom_call" | custom-call | tf_op jit(solution)/shard_map/products/pallas_call | solution.py:383

commit v2 on v1

--- a/solution.py
+++ b/solution.py
@@ -14,32 +14,39 @@
 
 
 def dispatch_kernel(
-    tok_ref, cot_ref, row_ref, col_ref, gate_ref, out_ref, send_ref, pick_ref, feed_ref, send_sem, recv_sem
+    tok_ref, cot_ref, route_ref, gate_ref, out_ref, send_ref, pick_ref, feed_ref, relay_ref,
+    send_sem, recv_sem, pass_send, pass_recv,
 ):
     tokens, width = tok_ref.shape
     fine = width // 4
     groups = out_ref.shape[0] // BLOCK
     experts = groups // 4
-    me, half = lax.axis_index("fsdp"), lax.axis_index("tp")
-    source_half = (me % 4) // 2
-    keeps_own = source_half == half
+    me, high = lax.axis_index("fsdp"), lax.axis_index("tp")
+    z, low, x, core = me // 16, (me // 8) % 2, (me // 2) % 4, me % 2
+    y = high * 2 + low
+
+    def plane(to_z, to_y):
+        return to_z * 16 + (to_y % 2) * 8 + x * 2 + core, to_y // 2
+
+    def beside(to_x, to_core):
+        return me - x * 2 - core + to_x * 2 + to_core, high
 
     barrier = pltpu.get_barrier_semaphore()
-
-    def greet(other, carry):
-        @pl.when(jnp.logical_or(other != me, source_half != half))
-        def _():
-            pl.semaphore_signal(barrier, inc=1, device_id=(other, source_half), device_id_type=MESH)
-
-        return carry
-
-    lax.fori_loop(0, groups, greet, 0)
-
-    row, col = row_ref[...], col_ref[...]
+    for step in range(1, 16):
+        pl.semaphore_signal(
+            barrier, inc=1, device_id=plane((z + step // 4) % 4, (y + step % 4) % 4), device_id_type=MESH
+        )
+    for step in range(1, 8):
+        pl.semaphore_signal(
+            barrier, inc=1, device_id=beside((x + step // 2) % 4, (core + step) % 2), device_id_type=MESH
+        )
+
+    row = route_ref[...].astype(jnp.float32)
+    col = jnp.broadcast_to(row, (tokens, tokens)).T
     first = lax.broadcasted_iota(jnp.int32, (tokens, tokens), 0)
     second = lax.broadcasted_iota(jnp.int32, (tokens, tokens), 1)
     before = jnp.where((col == row) & (first < second), 1.0, 0.0)
-    slot = row.astype(jnp.float32) * CAPACITY + jnp.sum(before, axis=0, keepdims=True)
+    slot = row * CAPACITY + jnp.sum(before, axis=0, keepdims=True)
     key = jnp.concatenate([slot + 1024.0 * part for part in range(4)], axis=1)
     place = lax.broadcasted_iota(jnp.int32, (experts * BLOCK, 1), 0).astype(jnp.float32)
     expert = jnp.floor((place + 0.5) * (1.0 / BLOCK))
@@ -47,78 +54,120 @@
     part = jnp.floor((within + 0.5) * (1.0 / CAPACITY))
     wanted = expert * CAPACITY + (within - part * CAPACITY) + 1024.0 * part
     pick_ref[...] = jnp.where(wanted == key, 1.0, 0.0).astype(jnp.bfloat16)
-    weighted = (gate_ref[...] * cot_ref[...].astype(jnp.float32)).astype(jnp.bfloat16)
+    gate = jnp.broadcast_to(gate_ref[...], (tokens, tokens)).T[:, 0:1]
+    weighted = (gate * cot_ref[...].astype(jnp.float32)).astype(jnp.bfloat16)
     for piece in range(2):
         for side in range(2):
             lanes = slice((2 * piece + side) * fine, (2 * piece + side + 1) * fine)
             feed_ref[piece, pl.ds(side * tokens, tokens), :] = tok_ref[:, lanes]
             feed_ref[piece, pl.ds((2 + side) * tokens, tokens), :] = weighted[:, lanes]
 
-    pl.semaphore_wait(barrier, groups - jnp.where(keeps_own, 1, 0))
-
-    def remote(expert, piece, side, number):
-        target = 4 * expert + 2 * half + piece
-        return pltpu.make_async_remote_copy(
-            src_ref=send_ref.at[piece, pl.ds(pl.multiple_of(expert * BLOCK, BLOCK), BLOCK), :],
-            dst_ref=out_ref.at[pl.ds(pl.multiple_of(me * BLOCK, BLOCK), BLOCK), :],
-            send_sem=send_sem.at[number],
-            recv_sem=recv_sem.at[me],
-            device_id=(target, side),
-            device_id_type=MESH,
-        )
-
-    def numbered(step):
-        expert = (me // 4 + step) % experts
-        return expert
-
-    def send(step, carry):
-        expert = numbered(step)
-        base = pl.multiple_of(expert * BLOCK, BLOCK)
+    def gather(step, carry):
+        at = pl.ds(pl.multiple_of(step * 4 * BLOCK, 4 * BLOCK), 4 * BLOCK)
         for piece in range(2):
-            send_ref[piece, pl.ds(base, BLOCK), :] = jnp.dot(
-                pick_ref[pl.ds(base, BLOCK), :], feed_ref[piece], preferred_element_type=jnp.float32
+            send_ref[piece, at, :] = jnp.dot(
+                pick_ref[at, :], feed_ref[piece], preferred_element_type=jnp.float32
             ).astype(jnp.bfloat16)
-            for side in range(2):
-                target = 4 * expert + 2 * half + piece
-                here = jnp.logical_and(target == me, half == side)
-                number = step * 4 + piece * 2 + side
-
-                @pl.when(jnp.logical_not(here))
-                def _():
-                    remote(expert, piece, side, number).start()
-
-                @pl.when(here)
-                def _():
-                    pltpu.make_async_copy(
-                        send_ref.at[piece, pl.ds(base, BLOCK), :],
-                        out_ref.at[pl.ds(pl.multiple_of(me * BLOCK, BLOCK), BLOCK), :],
-                        recv_sem.at[me],
-                    ).start()
-
-        return carry
-
-    lax.fori_loop(0, experts, send, 0)
+        return carry
+
+    lax.fori_loop(0, experts // 4, gather, 0)
+    pl.semaphore_wait(barrier, 22)
+
+    def block(number, count=1):
+        return pl.ds(pl.multiple_of(number * BLOCK, BLOCK), count * BLOCK)
+
+    def pair_of(stage):
+        return (x // 2 + 1 + stage // 2) % 2, (core + stage) % 2
+
+    def moves(number):
+        stage, step = number // 16, number % 16
+        return stage, step % 4, (step // 4 + step) % 4
+
+    def outward(number):
+        stage, dz, dy = moves(number)
+        pair, to_core = pair_of(stage)
+        to_z, to_y = (z + dz) % 4, (y + dy) % 4
+        slot = stage * 16 + z * 4 + y
+        source = send_ref.at[to_core, block(to_z * 4 + (to_y % 2) * 2 + pair), :]
+        target = relay_ref.at[block(slot), :]
+        here = jnp.logical_and(dz == 0, dy == 0)
+        local_copy = lambda: pltpu.make_async_copy(source, target, recv_sem.at[slot])
+        remote_copy = lambda: pltpu.make_async_remote_copy(
+            src_ref=source, dst_ref=target, send_sem=send_sem.at[number], recv_sem=recv_sem.at[slot],
+            device_id=plane(to_z, to_y), device_id_type=MESH,
+        )
+        return here, local_copy, remote_copy
+
+    def along(number):
+        stage, dz, dy = moves(number)
+        pair, to_core = pair_of(stage)
+        from_z, from_y = (z + 4 - dz) % 4, (y + 4 - dy) % 4
+        slot = stage * 16 + from_z * 4 + from_y
+        origin = from_z * 16 + (from_y % 2) * 8 + x * 2 + core
+        to_x = pair * 2 + from_y // 2
+        source, target = relay_ref.at[block(slot), :], out_ref.at[block(origin), :]
+        here = jnp.logical_and(to_x == x, to_core == core)
+        local_copy = lambda: pltpu.make_async_copy(source, target, pass_recv.at[origin])
+        remote_copy = lambda: pltpu.make_async_remote_copy(
+            src_ref=source, dst_ref=target, send_sem=pass_send.at[number], recv_sem=pass_recv.at[origin],
+            device_id=beside(to_x, to_core), device_id_type=MESH,
+        )
+        return slot, here, local_copy, remote_copy
+
+    def send(number, carry):
+        here, local_copy, remote_copy = outward(number)
+
+        @pl.when(here)
+        def _():
+            local_copy().start()
+
+        @pl.when(jnp.logical_not(here))
+        def _():
+            remote_copy().start()
+
+        return carry
+
+    lax.fori_loop(0, groups, send, 0)
+
+    def forward(number, carry):
+        slot, here, local_copy, remote_copy = along(number)
+        landed = relay_ref.at[block(slot), :]
+        pltpu.make_async_copy(landed, landed, recv_sem.at[slot]).wait()
+
+        @pl.when(here)
+        def _():
+            local_copy().start()
+
+        @pl.when(jnp.logical_not(here))
+        def _():
+            remote_copy().start()
+
+        return carry
+
+    lax.fori_loop(0, groups, forward, 0)
 
     def drain(source, carry):
-        block = out_ref.at[pl.ds(pl.multiple_of(source * BLOCK, BLOCK), BLOCK), :]
-        pltpu.make_async_copy(block, block, recv_sem.at[source]).wait()
+        landed = out_ref.at[block(source), :]
+        pltpu.make_async_copy(landed, landed, pass_recv.at[source]).wait()
         return carry
 
     lax.fori_loop(0, groups, drain, 0)
 
-    def sent(step, carry):
-        expert = numbered(step)
-        for piece in range(2):
-            for side in range(2):
-                target = 4 * expert + 2 * half + piece
-
-                @pl.when(jnp.logical_not(jnp.logical_and(target == me, half == side)))
-                def _():
-                    remote(expert, piece, side, step * 4 + piece * 2 + side).wait_send()
-
-        return carry
-
-    lax.fori_loop(0, experts, sent, 0)
+    def sent(number, carry):
+        here, _, remote_copy = outward(number)
+        _, passed_here, _, passed_copy = along(number)
+
+        @pl.when(jnp.logical_not(here))
+        def _():
+            remote_copy().wait_send()
+
+        @pl.when(jnp.logical_not(passed_here))
+        def _():
+            passed_copy().wait_send()
+
+        return carry
+
+    lax.fori_loop(0, groups, sent, 0)
 
 
 def curvature(total, width):
@@ -338,19 +387,19 @@
         dispatch_kernel,
         name="dispatch",
         out_shape=jax.ShapeDtypeStruct((groups * BLOCK, width // 4), bf16),
-        in_specs=[SPACE] * 5,
+        in_specs=[SPACE] * 4,
         out_specs=HBM,
         scratch_shapes=[
             pltpu.VMEM((2, experts * BLOCK, width // 4), bf16),
             pltpu.VMEM((experts * BLOCK, 4 * count), bf16),
             pltpu.VMEM((2, 4 * count, width // 4), bf16),
-            pltpu.SemaphoreType.DMA((groups,)),
-            pltpu.SemaphoreType.DMA((groups,)),
-        ],
+            pltpu.VMEM((groups * BLOCK, width // 4), bf16),
+        ]
+        + [pltpu.SemaphoreType.DMA((groups,))] * 4,
         compiler_params=pltpu.CompilerParams(
             collective_id=0, has_side_effects=True, vmem_limit_bytes=VMEM_LIMIT
         ),
-    )(tokens, cotangent, routes.reshape(1, count), routes, gates)
+    )(tokens, cotangent, routes.reshape(1, count), gates.reshape(1, count))
 
     tok, cot, curved = pl.pallas_call(
         group_kernel,

time: 169 us -> 141 us (0.83)
  Pallas kernels: 166 us -> 139 us
  local copies, waits for them, and re-layouts: 2.78 us -> 0 us
    pallas_call x1, Pallas kernels: 81.6 us -> 54.9 us  [local(): pl.pallas_call(dispatch_kernel, name='dispatch', out_shape=jax.ShapeDtype...]
    unnamed x2 -> x0, local copies, waits for them, and re-layouts: 2.78 us -> none
where the time goes in v2:
time: 141 us; the launch traced here: 139 us
  Pallas kernels  139 us (99%)
    pallas_call x1, Pallas kernels, local(): pl.pallas_call(group_kernel, name='group', out_shape=(jax.ShapeDtypeStruc...  73.7 us
    pallas_call x1, Pallas kernels, local(): pl.pallas_call(dispatch_kernel, name='dispatch', out_shape=jax.ShapeDtype...  54.9 us
    pallas_call x1, Pallas kernels, local(): pl.pallas_call(product_kernel, name='products', grid=(chunks,), out_shape...  10.2 us

profile of v2, /device:TPU:1, one launch (start us, length us, event | category | flops | bytes accessed | tf_op | source)
XLA Modules:
  0.0 139.5 jit_solution(13566607317718354031)
XLA Ops:
  0.6 54.9 %dispatch.1.packed_ref = bf16[3072,512]{1,0:T(8,128)(2,1)} custom-call(bf16[128,2048]{1,0:T(8,128)(2,1)} %tok_ref.1, bf16[128,2048]{1,0:T(8,128)(2,1)} %cot_ref.1, s32[1,128]{1,0:T(1,128)} %bitcast.17, f32[1,128]{1,0:T(1,128)} %bitcast.18), custom_call_target="tpu_custom_call" | custom-call | tf_op jit(solution)/shard_map/dispatch/pallas_call | solution.py:386
  55.6 73.7 %group.1 = (bf16[768,1024]{1,0:T(8,128)(2,1)}, bf16[768,1024]{1,0:T(8,128)(2,1)}, bf16[6,768,384]{2,1,0:T(8,128)(2,1)}) custom-call(bf16[3072,512]{1,0:T(8,128)(2,1)} %dispatch.1.packed_ref, bf16[1024,768]{1,0:T(8,128)(2,1)} %bitcast.11, bf16[1024,768]{1,0:T(8,128)(2,1)} %bitcast.12, bf16[1024,768]{1,0:T(8,128)(2,1)} %bitcast.13, ...), custom_call_target="tpu_custom_call" | custom-call | tf_op jit(solution)/shard_map/group/pallas_call | solution.py:404
  129.3 10.2 %products.1 = (f32[1024,768]{1,0:T(8,128)}, f32[1024,768]{1,0:T(8,128)}, f32[768,1024]{1,0:T(8,128)}) custom-call(bf16[768,1024]{1,0:T(8,128)(2,1)} %get-tuple-element.9.tok_ref, bf16[768,1024]{1,0:T(8,128)(2,1)} %get-tuple-element.10.cot_ref, bf16[6,768,384]{2,1,0:T(8,128)(2,1)} %get-tuple-element.11.curved_ref), custom_call_target="tpu_custom_call" | custom-call | tf_op jit(solution)/shard_map/products/pallas_call | solution.py:432

commit v3 on v2

v3 whole, which is shorter than its diff:
```python
import jax
import jax.numpy as jnp
from jax import lax
from jax.experimental import pallas as pl
from jax.experimental.pallas import tpu as pltpu
from jax.sharding import PartitionSpec as P

MESH = pl.DeviceIdType.MESH
CAPACITY = 12
BLOCK = 4 * CAPACITY
VMEM_LIMIT = 60 * 1024 * 1024
SPACE = pl.BlockSpec(memory_space=pltpu.VMEM)
HBM = pl.BlockSpec(memory_space=pl.ANY)


def layer_kernel(
    mine_ref, cotan_ref, route_ref, weight_ref, gate_ref, up_ref, gdir_ref, udir_ref, down_ref, ddir_ref,
    flip_ref, cot_ref, curved_ref,
    send_ref, pick_ref, feed_ref, relay_ref, packed_ref, tok_ref,
    fwd_ref, bwd_ref, keep_ref, core_out, core_in, chip_keep, chip_out, chip_in,
    send_sem, recv_sem, pass_send, pass_recv,
    load_sem, core_send, core_recv, chip_send, chip_recv, back_send, back_recv, last_send, last_recv,
):
    tokens, width = mine_ref.shape
    fine = width // 4
    groups = packed_ref.shape[0] // BLOCK
    rows, depth = tok_ref.shape
    chunks, _, wide = curved_ref.shape
    slim = wide // 3
    units = 2 * chunks
    parted, halved, quarter = rows // 2, rows // 4, rows // 8
    experts = groups // 4
    me, high = lax.axis_index("fsdp"), lax.axis_index("tp")
    z, low, x, core = me // 16, (me // 8) % 2, (me // 2) % 4, me % 2
    y = high * 2 + low

    def plane(to_z, to_y):
        return to_z * 16 + (to_y % 2) * 8 + x * 2 + core, to_y // 2

    def beside(to_x, to_core):
        return me - x * 2 - core + to_x * 2 + to_core, high

    barrier = pltpu.get_barrier_semaphore()
    for step in range(1, 16):
        pl.semaphore_signal(
            barrier, inc=1, device_id=plane((z + step // 4) % 4, (y + step % 4) % 4), device_id_type=MESH
        )
    for step in range(1, 8):
        pl.semaphore_signal(
            barrier, inc=1, device_id=beside((x + step // 2) % 4, (core + step) % 2), device_id_type=MESH
        )

    def loads(chunk):
        at = slice(chunk * slim, (chunk + 1) * slim)
        pieces = [
            (ref.at[:, at], fwd_ref.at[chunk, :, pl.ds(place * slim, slim)])
            for place, ref in enumerate((gate_ref, up_ref, gdir_ref, udir_ref))
        ] + [
            (ref.at[at, :], bwd_ref.at[chunk, pl.ds(place * slim, slim), :])
            for place, ref in enumerate((down_ref, ddir_ref))
        ]
        return [
            pltpu.make_async_copy(source, target, load_sem.at[chunk, place])
            for place, (source, target) in enumerate(pieces)
        ]

    row = route_ref[...].astype(jnp.float32)
    col = jnp.broadcast_to(row, (tokens, tokens)).T
    first = lax.broadcasted_iota(jnp.int32, (tokens, tokens), 0)
    second = lax.broadcasted_iota(jnp.int32, (tokens, tokens), 1)
    before = jnp.where((col == row) & (first < second), 1.0, 0.0)
    slot = row * CAPACITY + jnp.sum(before, axis=0, keepdims=True)
    key = jnp.concatenate([slot + 1024.0 * part for part in range(4)], axis=1)
    place = lax.broadcasted_iota(jnp.int32, (experts * BLOCK, 1), 0).astype(jnp.float32)
    expert = jnp.floor((place + 0.5) * (1.0 / BLOCK))
    within = place - expert * BLOCK
    part = jnp.floor((within + 0.5) * (1.0 / CAPACITY))
    wanted = expert * CAPACITY + (within - part * CAPACITY) + 1024.0 * part
    pick_ref[...] = jnp.where(wanted == key, 1.0, 0.0).astype(jnp.bfloat16)
    gate = jnp.broadcast_to(weight_ref[...], (tokens, tokens)).T[:, 0:1]
    weighted = (gate * cotan_ref[...].astype(jnp.float32)).astype(jnp.bfloat16)
    for piece in range(2):
        for side in range(2):
            lanes = slice((2 * piece + side) * fine, (2 * piece + side + 1) * fine)
            feed_ref[piece, pl.ds(side * tokens, tokens), :] = mine_ref[:, lanes]
            feed_ref[piece, pl.ds((2 + side) * tokens, tokens), :] = weighted[:, lanes]

    def gather(step, carry):
        at = pl.ds(pl.multiple_of(step * 4 * BLOCK, 4 * BLOCK), 4 * BLOCK)
        for piece in range(2):
            send_ref[piece, at, :] = jnp.dot(
                pick_ref[at, :], feed_ref[piece], preferred_element_type=jnp.float32
            ).astype(jnp.bfloat16)
        return carry

    lax.fori_loop(0, experts // 4, gather, 0)
    pl.semaphore_wait(barrier, 22)

    def block(number, count=1):
        return pl.ds(pl.multiple_of(number * BLOCK, BLOCK), count * BLOCK)

    def pair_of(stage):
        return (x // 2 + 1 + stage // 2) % 2, (core + stage) % 2

    def moves(number):
        stage, step = number // 16, number % 16
        return stage, step % 4, (step // 4 + step) % 4

    def outward(number):
        stage, dz, dy = moves(number)
        pair, to_core = pair_of(stage)
        to_z, to_y = (z + dz) % 4, (y + dy) % 4
        slot = stage * 16 + z * 4 + y
        source = send_ref.at[to_core, block(to_z * 4 + (to_y % 2) * 2 + pair), :]
        target = relay_ref.at[block(slot), :]
        here = jnp.logical_and(dz == 0, dy == 0)
        local_copy = lambda: pltpu.make_async_copy(source, target, recv_sem.at[slot])
        remote_copy = lambda: pltpu.make_async_remote_copy(
            src_ref=source, dst_ref=target, send_sem=send_sem.at[number], recv_sem=recv_sem.at[slot],
            device_id=plane(to_z, to_y), device_id_type=MESH,
        )
        return here, local_copy, remote_copy

    def along(number):
        stage, dz, dy = moves(number)
        pair, to_core = pair_of(stage)
        from_z, from_y = (z + 4 - dz) % 4, (y + 4 - dy) % 4
        slot = stage * 16 + from_z * 4 + from_y
        origin = (stage // 2) * 32 + from_z * 8 + (from_y % 2) * 4 + (x % 2) * 2 + core
        to_x = pair * 2 + from_y // 2
        source, target = relay_ref.at[block(slot), :], packed_ref.at[block(origin), :]
        here = jnp.logical_and(to_x == x, to_core == core)
        local_copy = lambda: pltpu.make_async_copy(source, target, pass_recv.at[origin])
        remote_copy = lambda: pltpu.make_async_remote_copy(
            src_ref=source, dst_ref=target, send_sem=pass_send.at[number], recv_sem=pass_recv.at[origin],
            device_id=beside(to_x, to_core), device_id_type=MESH,
        )
        return slot, here, local_copy, remote_copy

    def send(number, carry):
        here, local_copy, remote_copy = outward(number)

        @pl.when(here)
        def _():
            local_copy().start()

        @pl.when(jnp.logical_not(here))
        def _():
            remote_copy().start()

        return carry

    lax.fori_loop(0, groups, send, 0)
    for chunk in range(chunks):
        for copy in loads(chunk):
            copy.start()

    def forward(number, carry):
        slot, here, local_copy, remote_copy = along(number)
        landed = relay_ref.at[block(slot), :]
        pltpu.make_async_copy(landed, landed, recv_sem.at[slot]).wait()

        @pl.when(here)
        def _():
            local_copy().start()

        @pl.when(jnp.logical_not(here))
        def _():
            remote_copy().start()

        return carry

    lax.fori_loop(0, groups, forward, 0)

    sort_rows = 4 * BLOCK
    left = lax.broadcasted_iota(jnp.int32, (sort_rows, 1), 0).astype(jnp.float32)
    part = jnp.floor((left + 0.5) * (1.0 / BLOCK))
    source = jnp.floor((left - part * BLOCK + 0.5) * (1.0 / CAPACITY))
    rest = left - part * BLOCK - source * CAPACITY
    wanted = source * BLOCK + part * CAPACITY + rest
    have = lax.broadcasted_iota(jnp.int32, (1, sort_rows), 1).astype(jnp.float32)
    sorter = jnp.where(wanted == have, 1.0, 0.0).astype(jnp.bfloat16)

    def sort(group, carry):
        for number in range(4):
            landed = packed_ref.at[block(group * 4 + number), :]
            pltpu.make_async_copy(landed, landed, pass_recv.at[group * 4 + number]).wait()
        taken = packed_ref[pl.ds(pl.multiple_of(group * sort_rows, sort_rows), sort_rows), :]
        ordered = jnp.dot(sorter, taken, preferred_element_type=jnp.float32).astype(jnp.bfloat16)
        to = pl.ds(pl.multiple_of(group * BLOCK, BLOCK), BLOCK)
        tok_ref[to, 0:fine] = ordered[0:BLOCK]
        tok_ref[to, fine:depth] = ordered[BLOCK : 2 * BLOCK]
        cot_ref[to, 0:fine] = ordered[2 * BLOCK : 3 * BLOCK]
        cot_ref[to, fine:depth] = ordered[3 * BLOCK : 4 * BLOCK]
        return carry


    against = (((1,), (1,)), ((), ()))

    chip = x % 2
    core_mate, chip_mate = beside(x, 1 - core), beside(x + 1 - 2 * chip, core)

    def to_core(unit):
        slot = unit % 4
        return pltpu.make_async_remote_copy(
            src_ref=core_out.at[slot], dst_ref=core_in.at[unit],
            send_sem=core_send.at[unit], recv_sem=core_recv.at[unit],
            device_id=core_mate, device_id_type=MESH,
        )

    def to_chip(unit):
        return pltpu.make_async_remote_copy(
            src_ref=chip_out.at[unit], dst_ref=chip_in.at[unit],
            send_sem=chip_send.at[unit], recv_sem=chip_recv.at[unit],
            device_id=chip_mate, device_id_type=MESH,
        )

    def back(unit, where):
        begin = unit // chunks * parted + core * halved + where * quarter
        place = curved_ref.at[unit % chunks, pl.ds(pl.multiple_of(begin, quarter), quarter), :]
        return pltpu.make_async_remote_copy(
            src_ref=place, dst_ref=place,
            send_sem=back_send.at[unit], recv_sem=back_recv.at[unit],
            device_id=chip_mate, device_id_type=MESH,
        )

    def last(unit, where):
        begin = unit // chunks * parted + where * halved
        place = curved_ref.at[unit % chunks, pl.ds(pl.multiple_of(begin, halved), halved), :]
        return pltpu.make_async_remote_copy(
            src_ref=place, dst_ref=place,
            send_sem=last_send.at[unit], recv_sem=last_recv.at[unit],
            device_id=core_mate, device_id_type=MESH,
        )

    def forward_products(unit, whose, into, slot):
        chunk = unit % chunks
        begin = unit // chunks * parted + whose * halved
        at = pl.ds(pl.multiple_of(begin, halved), halved)
        into[slot, :, 0 : 4 * slim] = jnp.dot(
            tok_ref[at, :], fwd_ref[chunk], preferred_element_type=jnp.float32
        )
        into[slot, :, 4 * slim : 6 * slim] = lax.dot_general(
            cot_ref[at, :], bwd_ref[chunk], against, preferred_element_type=jnp.float32
        )

    def products(unit):
        @pl.when(unit < chunks)
        def _():
            for place in range(6):
                loaded = (
                    bwd_ref.at[unit, pl.ds(0, slim), :] if place >= 4 else fwd_ref.at[unit, :, pl.ds(0, slim)]
                )
                pltpu.make_async_copy(loaded, loaded, load_sem.at[unit, place]).wait()

        @pl.when(unit >= 4)
        def _():
            to_core(unit - 4).wait_send()

        forward_products(unit, 1 - core, core_out, unit % 4)
        to_core(unit).start()
        forward_products(unit, core, keep_ref, unit % 2)

    def core_sum(unit):
        to_core(unit).wait_recv()
        slot = unit % 2
        theirs = pl.ds(pl.multiple_of((1 - chip) * quarter, quarter), quarter)
        chip_out[unit] = (keep_ref[slot, theirs, :] + core_in[unit, theirs, :]).astype(jnp.bfloat16)
        to_chip(unit).start()
        ours = pl.ds(pl.multiple_of(chip * quarter, quarter), quarter)
        chip_keep[unit] = keep_ref[slot, ours, :] + core_in[unit, ours, :]

    def first_pass(step, carry):
        @pl.when(step % chunks == 0)
        def _():
            @pl.when(step < units)
            def _():
                lax.fori_loop(step // chunks * 8, step // chunks * 8 + 8, sort, 0)

        @pl.when(step < units)
        def _():
            products(step)

        @pl.when(step > 0)
        def _():
            core_sum(step - 1)

        return carry

    lax.fori_loop(0, units + 1, first_pass, 0)
    flip_ref[...] = tok_ref[...].T

    def curve(unit, carry):
        to_chip(unit).wait_recv()
        total = chip_keep[unit] + chip_in[unit].astype(jnp.float32)
        begin = unit // chunks * parted + core * halved + chip * quarter
        curved_ref[unit % chunks, pl.ds(pl.multiple_of(begin, quarter), quarter), :] = curvature(total, slim)
        back(unit, chip).start()
        return carry

    lax.fori_loop(0, units, curve, 0)

    def spread(unit, carry):
        back(unit, 1 - chip).wait_recv()
        last(unit, core).start()
        return carry

    lax.fori_loop(0, units, spread, 0)

    def finish(unit, carry):
        last(unit, 1 - core).wait_recv()

        @pl.when(unit >= units - 4)
        def _():
            to_core(unit).wait_send()

        to_chip(unit).wait_send()
        back(unit, chip).wait_send()
        last(unit, core).wait_send()
        return carry

    lax.fori_loop(0, units, finish, 0)
    def sent(number, carry):
        here, _, remote_copy = outward(number)
        _, passed_here, _, passed_copy = along(number)

        @pl.when(jnp.logical_not(here))
        def _():
            remote_copy().wait_send()

        @pl.when(jnp.logical_not(passed_here))
        def _():
            passed_copy().wait_send()

        return carry

    lax.fori_loop(0, groups, sent, 0)


def curvature(total, width):
    gate_pre, up_pre, gate_tan, up_tan, grad_hidden, tan_grad = (
        total[:, width * place : width * (place + 1)] for place in range(6)
    )
    sigmoid_gate = jax.nn.sigmoid(gate_pre)
    silu_gate = gate_pre * sigmoid_gate
    slope = sigmoid_gate * (1.0 + gate_pre * (1.0 - sigmoid_gate))
    bend = sigmoid_gate * (1.0 - sigmoid_gate) * (2.0 + gate_pre * (1.0 - 2.0 * sigmoid_gate))
    tan_gate = (
        tan_grad * up_pre * slope
        + grad_hidden * up_tan * slope
        + grad_hidden * up_pre * bend * gate_tan
    )
    tan_up = tan_grad * silu_gate + grad_hidden * slope * gate_tan
    tan_hidden = slope * gate_tan * up_pre + silu_gate * up_tan
    return jnp.concatenate([tan_gate, tan_up, tan_hidden], axis=1).astype(jnp.bfloat16)


def product_kernel(flip_ref, cot_ref, curved_ref, gate_out, up_out, down_out):
    slim = curved_ref.shape[2] // 3

    both = jnp.dot(flip_ref[...], curved_ref[0, :, 0 : 2 * slim], preferred_element_type=jnp.float32)
    gate_out[...] = both[:, 0:slim]
    up_out[...] = both[:, slim : 2 * slim]
    down_out[...] = lax.dot_general(
        curved_ref[0, :, 2 * slim : 3 * slim],
        cot_ref[...],
        (((0,), (0,)), ((), ())),
        preferred_element_type=jnp.float32,
    )


def local(
    tokens, cotangent, routes, gates, gate_proj, up_proj, down_proj, gate_dir, up_dir, down_dir
):
    count, width = tokens.shape
    groups = lax.axis_size("fsdp")
    experts = groups // 4
    depth, hidden = gate_proj.shape[1:]
    rows = groups * CAPACITY
    slim = 128
    chunks = hidden // slim
    bf16, f32 = jnp.bfloat16, jnp.float32

    units = 2 * chunks
    flipped, cot, curved = pl.pallas_call(
        layer_kernel,
        name="layer",
        out_shape=(
            jax.ShapeDtypeStruct((depth, rows), bf16),
            jax.ShapeDtypeStruct((rows, depth), bf16),
            jax.ShapeDtypeStruct((chunks, rows, 3 * slim), bf16),
        ),
        in_specs=[SPACE] * 4 + [HBM] * 6,
        out_specs=(SPACE,) * 3,
        scratch_shapes=[
            pltpu.VMEM((2, experts * BLOCK, width // 4), bf16),
            pltpu.VMEM((experts * BLOCK, 4 * count), bf16),
            pltpu.VMEM((2, 4 * count, width // 4), bf16),
            pltpu.VMEM((groups * BLOCK, width // 4), bf16),
            pltpu.VMEM((groups * BLOCK, width // 4), bf16),
            pltpu.VMEM((rows, depth), bf16),
            pltpu.VMEM((chunks, depth, 4 * slim), bf16),
            pltpu.VMEM((chunks, 2 * slim, depth), bf16),
            pltpu.VMEM((2, rows // 4, 6 * slim), f32),
            pltpu.VMEM((4, rows // 4, 6 * slim), f32),
            pltpu.VMEM((units, rows // 4, 6 * slim), f32),
            pltpu.VMEM((units, rows // 8, 6 * slim), f32),
            pltpu.VMEM((units, rows // 8, 6 * slim), bf16),
            pltpu.VMEM((units, rows // 8, 6 * slim), bf16),
        ]
        + [pltpu.SemaphoreType.DMA((groups,))] * 4
        + [pltpu.SemaphoreType.DMA((chunks, 6))]
        + [pltpu.SemaphoreType.DMA((units,))] * 8,
        compiler_params=pltpu.CompilerParams(
            collective_id=0, has_side_effects=True, vmem_limit_bytes=VMEM_LIMIT
        ),
    )(
        tokens, cotangent, routes.reshape(1, count), gates.reshape(1, count),
        gate_proj[0], up_proj[0], gate_dir[0], up_dir[0], down_proj[0], down_dir[0],
    )

    whole = lambda chunk: (0, 0)
    hess_gate, hess_up, hess_down = pl.pallas_call(
        product_kernel,
        name="products",
        grid=(chunks,),
        out_shape=(
            jax.ShapeDtypeStruct((depth, hidden), f32),
            jax.ShapeDtypeStruct((depth, hidden), f32),
            jax.ShapeDtypeStruct((hidden, depth), f32),
        ),
        in_specs=[
            pl.BlockSpec((depth, rows), whole),
            pl.BlockSpec((rows, depth), whole),
            pl.BlockSpec((1, rows, 3 * slim), lambda chunk: (chunk, 0, 0)),
        ],
        out_specs=(
            pl.BlockSpec((depth, slim), lambda chunk: (0, chunk)),
            pl.BlockSpec((depth, slim), lambda chunk: (0, chunk)),
            pl.BlockSpec((slim, depth), lambda chunk: (chunk, 0)),
        ),
        compiler_params=pltpu.CompilerParams(vmem_limit_bytes=VMEM_LIMIT),
    )(flipped, cot, curved)
    return (hess_gate[None], hess_up[None], hess_down[None])


def solution(mesh):
    return jax.shard_map(
        local,
        mesh=mesh,
        in_specs=(
            P("fsdp", "tp"),
            P("fsdp", "tp"),
            P("fsdp", None),
            P("fsdp", None),
            P("fsdp", None, "tp"),
            P("fsdp", None, "tp"),
            P("fsdp", "tp", None),
            P("fsdp", None, "tp"),
            P("fsdp", None, "tp"),
            P("fsdp", "tp", None),
        ),
        out_specs=(P("fsdp", None, "tp"), P("fsdp", None, "tp"), P("fsdp", "tp", None)),
        check_vma=False,
    )
```

time: 141 us -> 132 us (0.936); the launches traced: 139 us -> 132 us
  Pallas kernels: 139 us -> 131 us
    pallas_call x2 -> x1, Pallas kernels: 129 us -> 122 us  [local(): pl.pallas_call(layer_kernel, name='layer', out_shape=(jax.ShapeDtypeStruc...]
where the time goes in v3:
time: 132 us
  Pallas kernels  131 us (99%)
    pallas_call x1, Pallas kernels, local(): pl.pallas_call(layer_kernel, name='layer', out_shape=(jax.ShapeDtypeStruc...  122 us
    pallas_call x1, Pallas kernels, local(): pl.pallas_call(product_kernel, name='products', grid=(chunks,), out_shape...  9.75 us

profile of v3, /device:TPU:1, one launch (start us, length us, event | category | flops | bytes accessed | tf_op | source)
XLA Modules:
  0.0 132.1 jit_solution(4166348699113561138)
XLA Ops:
  0.6 121.7 %layer.1 = (bf16[1024,768]{1,0:T(8,128)(2,1)}, bf16[768,1024]{1,0:T(8,128)(2,1)}, bf16[6,768,384]{2,1,0:T(8,128)(2,1)}) custom-call(bf16[128,2048]{1,0:T(8,128)(2,1)} %mine_ref.1, bf16[128,2048]{1,0:T(8,128)(2,1)} %cotan_ref.1, s32[1,128]{1,0:T(1,128)} %bitcast.17, f32[1,128]{1,0:T(1,128)} %bitcast.18, bf16[1024,768]{1,0:T(8,128)(2,1)} %bitcast.11, ...), custom_call_target="tpu_custom_call" | custom-call | tf_op jit(solution)/shard_map/layer/pallas_call | solution.py:385
  122.4 9.7 %products.1 = (f32[1024,768]{1,0:T(8,128)}, f32[1024,768]{1,0:T(8,128)}, f32[768,1024]{1,0:T(8,128)}) custom-call(bf16[1024,768]{1,0:T(8,128)(2,1)} %get-tuple-element.9.flip_ref, bf16[768,1024]{1,0:T(8,128)(2,1)} %get-tuple-element.10.cot_ref, bf16[6,768,384]{2,1,0:T(8,128)(2,1)} %get-tuple-element.11.curved_ref), custom_call_target="tpu_custom_call" | custom-call | tf_op jit(solution)/shard_map/products/pallas_call | solution.py:423

commit v4 on v3

--- a/solution.py
+++ b/solution.py
@@ -16,23 +16,24 @@
 def layer_kernel(
     mine_ref, cotan_ref, route_ref, weight_ref, gate_ref, up_ref, gdir_ref, udir_ref, down_ref, ddir_ref,
     flip_ref, cot_ref, curved_ref,
-    send_ref, pick_ref, feed_ref, relay_ref, packed_ref, tok_ref,
-    fwd_ref, bwd_ref, keep_ref, core_out, core_in, chip_keep, chip_out, chip_in,
-    send_sem, recv_sem, pass_send, pass_recv,
+    send_ref, pick_ref, feed_ref, first_ref, second_ref, packed_ref, tok_ref,
+    fwd_ref, bwd_ref, part_ref, core_in, chip_keep, chip_out, chip_in,
+    z_send, z_recv, x_send, x_recv, y_send, y_recv,
     load_sem, core_send, core_recv, chip_send, chip_recv, back_send, back_recv, last_send, last_recv,
 ):
     tokens, width = mine_ref.shape
     fine = width // 4
-    groups = packed_ref.shape[0] // BLOCK
     rows, depth = tok_ref.shape
     chunks, _, wide = curved_ref.shape
     slim = wide // 3
-    units = 2 * chunks
-    parted, halved, quarter = rows // 2, rows // 4, rows // 8
-    experts = groups // 4
+    parts = packed_ref.shape[0] // 4
+    units = parts * chunks
+    parted, halved, quarter = rows // parts, rows // parts // 2, rows // parts // 4
+    experts = 4 * parts
     me, high = lax.axis_index("fsdp"), lax.axis_index("tp")
     z, low, x, core = me // 16, (me // 8) % 2, (me // 2) % 4, me % 2
     y = high * 2 + low
+    facing = y + core * (3 - 2 * y)
 
     def plane(to_z, to_y):
         return to_z * 16 + (to_y % 2) * 8 + x * 2 + core, to_y // 2
@@ -41,10 +42,9 @@
         return me - x * 2 - core + to_x * 2 + to_core, high
 
     barrier = pltpu.get_barrier_semaphore()
-    for step in range(1, 16):
-        pl.semaphore_signal(
-            barrier, inc=1, device_id=plane((z + step // 4) % 4, (y + step % 4) % 4), device_id_type=MESH
-        )
+    for step in range(1, 4):
+        for there in (plane((z + step) % 4, facing), plane(z, (y + step) % 4)):
+            pl.semaphore_signal(barrier, inc=1, device_id=there, device_id_type=MESH)
     for step in range(1, 8):
         pl.semaphore_signal(
             barrier, inc=1, device_id=beside((x + step // 2) % 4, (core + step) % 2), device_id_type=MESH
@@ -72,8 +72,11 @@
     slot = row * CAPACITY + jnp.sum(before, axis=0, keepdims=True)
     key = jnp.concatenate([slot + 1024.0 * part for part in range(4)], axis=1)
     place = lax.broadcasted_iota(jnp.int32, (experts * BLOCK, 1), 0).astype(jnp.float32)
-    expert = jnp.floor((place + 0.5) * (1.0 / BLOCK))
-    within = place - expert * BLOCK
+    number = jnp.floor((place + 0.5) * (1.0 / BLOCK))
+    within = place - number * BLOCK
+    span = jnp.floor((number + 0.5) * 0.25)
+    pair = jnp.floor((number - 4.0 * span + 0.5) * 0.5)
+    expert = 2.0 * number - 4.0 * span - 3.0 * pair
     part = jnp.floor((within + 0.5) * (1.0 / CAPACITY))
     wanted = expert * CAPACITY + (within - part * CAPACITY) + 1024.0 * part
     pick_ref[...] = jnp.where(wanted == key, 1.0, 0.0).astype(jnp.bfloat16)
@@ -88,89 +91,91 @@
     def gather(step, carry):
         at = pl.ds(pl.multiple_of(step * 4 * BLOCK, 4 * BLOCK), 4 * BLOCK)
         for piece in range(2):
-            send_ref[piece, at, :] = jnp.dot(
-                pick_ref[at, :], feed_ref[piece], preferred_element_type=jnp.float32
-            ).astype(jnp.bfloat16)
-        return carry
-
-    lax.fori_loop(0, experts // 4, gather, 0)
-    pl.semaphore_wait(barrier, 22)
-
-    def block(number, count=1):
-        return pl.ds(pl.multiple_of(number * BLOCK, BLOCK), count * BLOCK)
-
-    def pair_of(stage):
-        return (x // 2 + 1 + stage // 2) % 2, (core + stage) % 2
-
-    def moves(number):
-        stage, step = number // 16, number % 16
-        return stage, step % 4, (step // 4 + step) % 4
-
-    def outward(number):
-        stage, dz, dy = moves(number)
-        pair, to_core = pair_of(stage)
-        to_z, to_y = (z + dz) % 4, (y + dy) % 4
-        slot = stage * 16 + z * 4 + y
-        source = send_ref.at[to_core, block(to_z * 4 + (to_y % 2) * 2 + pair), :]
-        target = relay_ref.at[block(slot), :]
-        here = jnp.logical_and(dz == 0, dy == 0)
-        local_copy = lambda: pltpu.make_async_copy(source, target, recv_sem.at[slot])
-        remote_copy = lambda: pltpu.make_async_remote_copy(
-            src_ref=source, dst_ref=target, send_sem=send_sem.at[number], recv_sem=recv_sem.at[slot],
-            device_id=plane(to_z, to_y), device_id_type=MESH,
-        )
-        return here, local_copy, remote_copy
-
-    def along(number):
-        stage, dz, dy = moves(number)
-        pair, to_core = pair_of(stage)
-        from_z, from_y = (z + 4 - dz) % 4, (y + 4 - dy) % 4
-        slot = stage * 16 + from_z * 4 + from_y
-        origin = (stage // 2) * 32 + from_z * 8 + (from_y % 2) * 4 + (x % 2) * 2 + core
-        to_x = pair * 2 + from_y // 2
-        source, target = relay_ref.at[block(slot), :], packed_ref.at[block(origin), :]
-        here = jnp.logical_and(to_x == x, to_core == core)
-        local_copy = lambda: pltpu.make_async_copy(source, target, pass_recv.at[origin])
-        remote_copy = lambda: pltpu.make_async_remote_copy(
-            src_ref=source, dst_ref=target, send_sem=pass_send.at[number], recv_sem=pass_recv.at[origin],
-            device_id=beside(to_x, to_core), device_id_type=MESH,
-        )
-        return slot, here, local_copy, remote_copy
-
-    def send(number, carry):
-        here, local_copy, remote_copy = outward(number)
-
-        @pl.when(here)
-        def _():
-            local_copy().start()
-
-        @pl.when(jnp.logical_not(here))
-        def _():
-            remote_copy().start()
-
-        return carry
-
-    lax.fori_loop(0, groups, send, 0)
+            picked = jnp.dot(pick_ref[at, :], feed_ref[piece], preferred_element_type=jnp.float32)
+            for place in range(4):
+                send_ref[piece, step, place // 2, place % 2] = picked[
+                    place * BLOCK : (place + 1) * BLOCK
+                ].astype(jnp.bfloat16)
+        return carry
+
+    lax.fori_loop(0, parts, gather, 0)
+    pl.semaphore_wait(barrier, 13)
+
+    def transfer(here, source, target, send_sem, recv_sem, device):
+        def start():
+            @pl.when(here)
+            def _():
+                pltpu.make_async_copy(source, target, recv_sem).start()
+
+            @pl.when(jnp.logical_not(here))
+            def _():
+                remote().start()
+
+        def remote():
+            return pltpu.make_async_remote_copy(
+                src_ref=source, dst_ref=target, send_sem=send_sem, recv_sem=recv_sem,
+                device_id=device, device_id_type=MESH,
+            )
+
+        def finish():
+            @pl.when(jnp.logical_not(here))
+            def _():
+                remote().wait_send()
+
+        return start, finish
+
+    def landed(place, sem):
+        pltpu.make_async_copy(place, place, sem).wait()
+
+    def along_z(part, to_core):
+        dz = part + part // 2 * (1 - 2 * (part % 2))
+        to_z = (z + dz) % 4
+        return transfer(
+            jnp.logical_and(dz == 0, core == 0), send_ref.at[to_core, to_z], first_ref.at[part, to_core],
+            z_send.at[part * 2 + to_core], z_recv.at[part * 2 + to_core], plane(to_z, facing),
+        )
+
+    def along_x(part, pair, to_core):
+        to_x = pair * 2 + (high + core) % 2
+        return transfer(
+            jnp.logical_and(to_x == x, to_core == core),
+            first_ref.at[part, to_core, pair],
+            second_ref.at[part, :, pl.ds(pl.multiple_of(x * BLOCK, BLOCK), BLOCK), :],
+            x_send.at[part * 4 + pair * 2 + to_core], x_recv.at[part * 4 + x], beside(to_x, to_core),
+        )
+
+    def along_y(part, to_low, to_high):
+        to_y = to_high * 2 + to_low
+        origin_core = (high + x) % 2
+        origin = (low + origin_core * (1 - 2 * low)) * 2 + origin_core
+        return transfer(
+            to_y == y, second_ref.at[part, to_low], packed_ref.at[part * 4 + origin],
+            y_send.at[part * 4 + to_y], y_recv.at[part * 4 + origin], plane(z, to_y),
+        )
+
+    def hop_z(part, carry):
+        for to_core in range(2):
+            along_z(part, to_core)[0]()
+        return carry
+
+    def hop_x(part):
+        for to_core in range(2):
+            landed(first_ref.at[part, to_core], z_recv.at[part * 2 + to_core])
+        for pair in range(2):
+            for to_core in range(2):
+                along_x(part, pair, to_core)[0]()
+
+    def hop_y(part):
+        for number in range(4):
+            landed(second_ref.at[part, :, pl.ds(number * BLOCK, BLOCK), :], x_recv.at[part * 4 + number])
+        for to_low in range(2):
+            for to_high in range(2):
+                along_y(part, to_low, to_high)[0]()
+
+    lax.fori_loop(0, parts, hop_z, 0)
     for chunk in range(chunks):
         for copy in loads(chunk):
             copy.start()
-
-    def forward(number, carry):
-        slot, here, local_copy, remote_copy = along(number)
-        landed = relay_ref.at[block(slot), :]
-        pltpu.make_async_copy(landed, landed, recv_sem.at[slot]).wait()
-
-        @pl.when(here)
-        def _():
-            local_copy().start()
-
-        @pl.when(jnp.logical_not(here))
-        def _():
-            remote_copy().start()
-
-        return carry
-
-    lax.fori_loop(0, groups, forward, 0)
 
     sort_rows = 4 * BLOCK
     left = lax.broadcasted_iota(jnp.int32, (sort_rows, 1), 0).astype(jnp.float32)
@@ -182,10 +187,8 @@
     sorter = jnp.where(wanted == have, 1.0, 0.0).astype(jnp.bfloat16)
 
     def sort(group, carry):
-        for number in range(4):
-            landed = packed_ref.at[block(group * 4 + number), :]
-            pltpu.make_async_copy(landed, landed, pass_recv.at[group * 4 + number]).wait()
-        taken = packed_ref[pl.ds(pl.multiple_of(group * sort_rows, sort_rows), sort_rows), :]
+        landed(packed_ref.at[group], y_recv.at[group])
+        taken = packed_ref[group]
         ordered = jnp.dot(sorter, taken, preferred_element_type=jnp.float32).astype(jnp.bfloat16)
         to = pl.ds(pl.multiple_of(group * BLOCK, BLOCK), BLOCK)
         tok_ref[to, 0:fine] = ordered[0:BLOCK]
@@ -201,9 +204,9 @@
     core_mate, chip_mate = beside(x, 1 - core), beside(x + 1 - 2 * chip, core)
 
     def to_core(unit):
-        slot = unit % 4
+        theirs = pl.ds(pl.multiple_of((1 - core) * halved, halved), halved)
         return pltpu.make_async_remote_copy(
-            src_ref=core_out.at[slot], dst_ref=core_in.at[unit],
+            src_ref=part_ref.at[unit % 4, theirs, :], dst_ref=core_in.at[unit],
             send_sem=core_send.at[unit], recv_sem=core_recv.at[unit],
             device_id=core_mate, device_id_type=MESH,
         )
@@ -233,17 +236,6 @@
             device_id=core_mate, device_id_type=MESH,
         )
 
-    def forward_products(unit, whose, into, slot):
-        chunk = unit % chunks
-        begin = unit // chunks * parted + whose * halved
-        at = pl.ds(pl.multiple_of(begin, halved), halved)
-        into[slot, :, 0 : 4 * slim] = jnp.dot(
-            tok_ref[at, :], fwd_ref[chunk], preferred_element_type=jnp.float32
-        )
-        into[slot, :, 4 * slim : 6 * slim] = lax.dot_general(
-            cot_ref[at, :], bwd_ref[chunk], against, preferred_element_type=jnp.float32
-        )
-
     def products(unit):
         @pl.when(unit < chunks)
         def _():
@@ -257,38 +249,43 @@
         def _():
             to_core(unit - 4).wait_send()
 
-        forward_products(unit, 1 - core, core_out, unit % 4)
+        chunk = unit % chunks
+        at = pl.ds(pl.multiple_of(unit // chunks * parted, parted), parted)
+        part_ref[unit % 4, :, 0 : 4 * slim] = jnp.dot(
+            tok_ref[at, :], fwd_ref[chunk], preferred_element_type=jnp.float32
+        )
+        part_ref[unit % 4, :, 4 * slim : 6 * slim] = lax.dot_general(
+            cot_ref[at, :], bwd_ref[chunk], against, preferred_element_type=jnp.float32
+        )
         to_core(unit).start()
-        forward_products(unit, core, keep_ref, unit % 2)
 
     def core_sum(unit):
         to_core(unit).wait_recv()
-        slot = unit % 2
-        theirs = pl.ds(pl.multiple_of((1 - chip) * quarter, quarter), quarter)
-        chip_out[unit] = (keep_ref[slot, theirs, :] + core_in[unit, theirs, :]).astype(jnp.bfloat16)
+        slot = unit % 4
+
+        def whole(where):
+            own = pl.ds(pl.multiple_of(core * halved + where * quarter, quarter), quarter)
+            return part_ref[slot, own, :] + core_in[unit, pl.ds(pl.multiple_of(where * quarter, quarter), quarter), :]
+
+        chip_out[unit] = whole(1 - chip).astype(jnp.bfloat16)
         to_chip(unit).start()
-        ours = pl.ds(pl.multiple_of(chip * quarter, quarter), quarter)
-        chip_keep[unit] = keep_ref[slot, ours, :] + core_in[unit, ours, :]
-
-    def first_pass(step, carry):
-        @pl.when(step % chunks == 0)
-        def _():
-            @pl.when(step < units)
+        chip_keep[unit] = whole(chip)
+
+    def partial_products(part):
+        lax.fori_loop(part * 4, part * 4 + 4, sort, 0)
+
+        def both(step, carry):
+            @pl.when(step < chunks)
             def _():
-                lax.fori_loop(step // chunks * 8, step // chunks * 8 + 8, sort, 0)
-
-        @pl.when(step < units)
-        def _():
-            products(step)
-
-        @pl.when(step > 0)
-        def _():
-            core_sum(step - 1)
-
-        return carry
-
-    lax.fori_loop(0, units + 1, first_pass, 0)
-    flip_ref[...] = tok_ref[...].T
+                products(part * chunks + step)
+
+            @pl.when(step > 0)
+            def _():
+                core_sum(part * chunks + step - 1)
+
+            return carry
+
+        lax.fori_loop(0, chunks + 1, both, 0)
 
     def curve(unit, carry):
         to_chip(unit).wait_recv()
@@ -298,7 +295,27 @@
         back(unit, chip).start()
         return carry
 
-    lax.fori_loop(0, units, curve, 0)
+    def advance(step, carry):
+        @pl.when(step < parts)
+        def _():
+            hop_x(step)
+
+        @pl.when(jnp.logical_and(step >= 1, step < parts + 1))
+        def _():
+            hop_y(step - 1)
+
+        @pl.when(jnp.logical_and(step >= 3, step < parts + 3))
+        def _():
+            partial_products(step - 3)
+
+        @pl.when(step >= 4)
+        def _():
+            lax.fori_loop((step - 4) * chunks, (step - 3) * chunks, curve, 0)
+
+        return carry
+
+    lax.fori_loop(0, parts + 4, advance, 0)
+    flip_ref[...] = tok_ref[...].T
 
     def spread(unit, carry):
         back(unit, 1 - chip).wait_recv()
@@ -320,21 +337,15 @@
         return carry
 
     lax.fori_loop(0, units, finish, 0)
-    def sent(number, carry):
-        here, _, remote_copy = outward(number)
-        _, passed_here, _, passed_copy = along(number)
-
-        @pl.when(jnp.logical_not(here))
-        def _():
-            remote_copy().wait_send()
-
-        @pl.when(jnp.logical_not(passed_here))
-        def _():
-            passed_copy().wait_send()
-
-        return carry
-
-    lax.fori_loop(0, groups, sent, 0)
+    def sent(part, carry):
+        for first in range(2):
+            along_z(part, first)[1]()
+            for second in range(2):
+                along_x(part, first, second)[1]()
+                along_y(part, first, second)[1]()
+        return carry
+
+    lax.fori_loop(0, parts, sent, 0)
 
 
 def curvature(total, width):
@@ -377,11 +388,13 @@
     experts = groups // 4
     depth, hidden = gate_proj.shape[1:]
     rows = groups * CAPACITY
-    slim = 128
+    slim = 256
     chunks = hidden // slim
     bf16, f32 = jnp.bfloat16, jnp.float32
 
-    units = 2 * chunks
+    parts = 4
+    units = parts * chunks
+    parted = rows // parts
     flipped, cot, curved = pl.pallas_call(
         layer_kernel,
         name="layer",
@@ -393,22 +406,23 @@
         in_specs=[SPACE] * 4 + [HBM] * 6,
         out_specs=(SPACE,) * 3,
         scratch_shapes=[
-            pltpu.VMEM((2, experts * BLOCK, width // 4), bf16),
+            pltpu.VMEM((2, 4, 2, 2, BLOCK, width // 4), bf16),
             pltpu.VMEM((experts * BLOCK, 4 * count), bf16),
             pltpu.VMEM((2, 4 * count, width // 4), bf16),
-            pltpu.VMEM((groups * BLOCK, width // 4), bf16),
-            pltpu.VMEM((groups * BLOCK, width // 4), bf16),
+            pltpu.VMEM((parts, 2, 2, 2, BLOCK, width // 4), bf16),
+            pltpu.VMEM((parts, 2, 4 * BLOCK, width // 4), bf16),
+            pltpu.VMEM((parts * 4, 4 * BLOCK, width // 4), bf16),
             pltpu.VMEM((rows, depth), bf16),
             pltpu.VMEM((chunks, depth, 4 * slim), bf16),
             pltpu.VMEM((chunks, 2 * slim, depth), bf16),
-            pltpu.VMEM((2, rows // 4, 6 * slim), f32),
-            pltpu.VMEM((4, rows // 4, 6 * slim), f32),
-            pltpu.VMEM((units, rows // 4, 6 * slim), f32),
-            pltpu.VMEM((units, rows // 8, 6 * slim), f32),
-            pltpu.VMEM((units, rows // 8, 6 * slim), bf16),
-            pltpu.VMEM((units, rows // 8, 6 * slim), bf16),
+            pltpu.VMEM((4, parted, 6 * slim), f32),
+            pltpu.VMEM((units, parted // 2, 6 * slim), f32),
+            pltpu.VMEM((units, parted // 4, 6 * slim), f32),
+            pltpu.VMEM((units, parted // 4, 6 * slim), bf16),
+            pltpu.VMEM((units, parted // 4, 6 * slim), bf16),
         ]
-        + [pltpu.SemaphoreType.DMA((groups,))] * 4
+        + [pltpu.SemaphoreType.DMA((parts * 2,))] * 2
+        + [pltpu.SemaphoreType.DMA((parts * 4,))] * 4
         + [pltpu.SemaphoreType.DMA((chunks, 6))]
         + [pltpu.SemaphoreType.DMA((units,))] * 8,
         compiler_params=pltpu.CompilerParams(

time: 132 us -> 125 us (0.947)
  Pallas kernels: 131 us -> 124 us
    pallas_call x1, Pallas kernels: 122 us -> 116 us  [local(): pl.pallas_call(layer_kernel, name='layer', out_shape=(jax.ShapeDtypeStruc...]
    pallas_call x1, Pallas kernels: 9.75 us -> 8.39 us  [local(): pl.pallas_call(product_kernel, name='products', grid=(chunks,), out_shape...]
where the time goes in v4:
time: 125 us
  Pallas kernels  124 us (99%)
    pallas_call x1, Pallas kernels, local(): pl.pallas_call(layer_kernel, name='layer', out_shape=(jax.ShapeDtypeStruc...  116 us
    pallas_call x1, Pallas kernels, local(): pl.pallas_call(product_kernel, name='products', grid=(chunks,), out_shape...  8.39 us

profile of v4, /device:TPU:1, one launch (start us, length us, event | category | flops | bytes accessed | tf_op | source)
XLA Modules:
  0.0 124.7 jit_solution(11058690151228435791)
XLA Ops:
  0.6 115.7 %layer.1 = (bf16[1024,768]{1,0:T(8,128)(2,1)}, bf16[768,1024]{1,0:T(8,128)(2,1)}, bf16[3,768,768]{2,1,0:T(8,128)(2,1)}) custom-call(bf16[128,2048]{1,0:T(8,128)(2,1)} %mine_ref.1, bf16[128,2048]{1,0:T(8,128)(2,1)} %cotan_ref.1, s32[1,128]{1,0:T(1,128)} %bitcast.17, f32[1,128]{1,0:T(1,128)} %bitcast.18, bf16[1024,768]{1,0:T(8,128)(2,1)} %bitcast.11, ...), custom_call_target="tpu_custom_call" | custom-call | tf_op jit(solution)/shard_map/layer/pallas_call | solution.py:398
  116.3 8.4 %products.1 = (f32[1024,768]{1,0:T(8,128)}, f32[1024,768]{1,0:T(8,128)}, f32[768,1024]{1,0:T(8,128)}) custom-call(bf16[1024,768]{1,0:T(8,128)(2,1)} %get-tuple-element.9.flip_ref, bf16[768,1024]{1,0:T(8,128)(2,1)} %get-tuple-element.10.cot_ref, bf16[3,768,768]{2,1,0:T(8,128)(2,1)} %get-tuple-element.11.curved_ref), custom_call_target="tpu_custom_call" | custom-call | tf_op jit(solution)/shard_map/products/pallas_call | solution.py:437

commit v5 on v4

--- a/solution.py
+++ b/solution.py
@@ -15,11 +15,11 @@
 
 def layer_kernel(
     mine_ref, cotan_ref, route_ref, weight_ref, gate_ref, up_ref, gdir_ref, udir_ref, down_ref, ddir_ref,
-    flip_ref, cot_ref, curved_ref,
-    send_ref, pick_ref, feed_ref, first_ref, second_ref, packed_ref, tok_ref,
+    flip_out, cot_out, curved_out,
+    flip_ref, cot_ref, curved_ref, send_ref, pick_ref, feed_ref, first_ref, second_ref, packed_ref, tok_ref,
     fwd_ref, bwd_ref, part_ref, core_in, chip_keep, chip_out, chip_in,
     z_send, z_recv, x_send, x_recv, y_send, y_recv,
-    load_sem, core_send, core_recv, chip_send, chip_recv, back_send, back_recv, last_send, last_recv,
+    load_sem, core_send, core_recv, chip_send, chip_recv, back_send, back_recv, last_send, last_recv, out_sem,
 ):
     tokens, width = mine_ref.shape
     fine = width // 4
@@ -172,7 +172,11 @@
             for to_high in range(2):
                 along_y(part, to_low, to_high)[0]()
 
-    lax.fori_loop(0, parts, hop_z, 0)
+    def arrive(part):
+        for number in range(4):
+            landed(packed_ref.at[part * 4 + number], y_recv.at[part * 4 + number])
+
+    lax.fori_loop(0, 2, hop_z, 0)
     for chunk in range(chunks):
         for copy in loads(chunk):
             copy.start()
@@ -187,7 +191,6 @@
     sorter = jnp.where(wanted == have, 1.0, 0.0).astype(jnp.bfloat16)
 
     def sort(group, carry):
-        landed(packed_ref.at[group], y_recv.at[group])
         taken = packed_ref[group]
         ordered = jnp.dot(sorter, taken, preferred_element_type=jnp.float32).astype(jnp.bfloat16)
         to = pl.ds(pl.multiple_of(group * BLOCK, BLOCK), BLOCK)
@@ -295,28 +298,57 @@
         back(unit, chip).start()
         return carry
 
+    def cross(step, carry):
+        hop_x(step)
+
+        @pl.when(step + 2 < parts)
+        def _():
+            hop_z(step + 2, 0)
+
+        @pl.when(step == 1)
+        def _():
+            hop_y(0)
+
+        return carry
+
+    lax.fori_loop(0, parts, cross, 0)
+
+    rows_out = [
+        pltpu.make_async_copy(flip_ref, flip_out, out_sem.at[units]),
+        pltpu.make_async_copy(cot_ref, cot_out, out_sem.at[units + 1]),
+    ]
+
+    def curved_copy(unit):
+        at = pl.ds(pl.multiple_of(unit // chunks * parted, parted), parted)
+        chunk = unit % chunks
+        return pltpu.make_async_copy(curved_ref.at[chunk, at, :], curved_out.at[chunk, at, :], out_sem.at[unit])
+
     def advance(step, carry):
         @pl.when(step < parts)
         def _():
-            hop_x(step)
-
-        @pl.when(jnp.logical_and(step >= 1, step < parts + 1))
-        def _():
-            hop_y(step - 1)
-
-        @pl.when(jnp.logical_and(step >= 3, step < parts + 3))
-        def _():
-            partial_products(step - 3)
-
-        @pl.when(step >= 4)
-        def _():
-            lax.fori_loop((step - 4) * chunks, (step - 3) * chunks, curve, 0)
-
-        return carry
-
-    lax.fori_loop(0, parts + 4, advance, 0)
-    flip_ref[...] = tok_ref[...].T
-
+            arrive(step)
+
+        @pl.when(step + 1 < parts)
+        def _():
+            hop_y(step + 1)
+
+        @pl.when(step == parts)
+        def _():
+            flip_ref[...] = tok_ref[...].T
+            for copy in rows_out:
+                copy.start()
+
+        @pl.when(step >= 2)
+        def _():
+            lax.fori_loop((step - 2) * chunks, (step - 2) * chunks + chunks, curve, 0)
+
+        @pl.when(step < parts)
+        def _():
+            partial_products(step)
+
+        return carry
+
+    lax.fori_loop(0, parts + 2, advance, 0)
     def spread(unit, carry):
         back(unit, 1 - chip).wait_recv()
         last(unit, core).start()
@@ -326,14 +358,15 @@
 
     def finish(unit, carry):
         last(unit, 1 - core).wait_recv()
-
-        @pl.when(unit >= units - 4)
-        def _():
-            to_core(unit).wait_send()
-
-        to_chip(unit).wait_send()
         back(unit, chip).wait_send()
         last(unit, core).wait_send()
+        curved_copy(unit).start()
+
+        @pl.when(unit >= units - 4)
+        def _():
+            to_core(unit).wait_send()
+
+        to_chip(unit).wait_send()
         return carry
 
     lax.fori_loop(0, units, finish, 0)
@@ -346,6 +379,14 @@
         return carry
 
     lax.fori_loop(0, parts, sent, 0)
+
+    def written(unit, carry):
+        curved_copy(unit).wait()
+        return carry
+
+    lax.fori_loop(0, units, written, 0)
+    for copy in rows_out:
+        copy.wait()
 
 
 def curvature(total, width):
@@ -366,18 +407,57 @@
     return jnp.concatenate([tan_gate, tan_up, tan_hidden], axis=1).astype(jnp.bfloat16)
 
 
-def product_kernel(flip_ref, cot_ref, curved_ref, gate_out, up_out, down_out):
-    slim = curved_ref.shape[2] // 3
-
-    both = jnp.dot(flip_ref[...], curved_ref[0, :, 0 : 2 * slim], preferred_element_type=jnp.float32)
-    gate_out[...] = both[:, 0:slim]
-    up_out[...] = both[:, slim : 2 * slim]
-    down_out[...] = lax.dot_general(
-        curved_ref[0, :, 2 * slim : 3 * slim],
-        cot_ref[...],
-        (((0,), (0,)), ((), ())),
-        preferred_element_type=jnp.float32,
-    )
+def product_kernel(
+    flip_in, cot_in, curved_in, gate_out, up_out, down_out,
+    flip_ref, cot_ref, curved_ref, gate_ref, up_ref, down_ref, load_sem, store_sem,
+):
+    chunks, _, wide = curved_ref.shape
+    slim = wide // 3
+    half = flip_ref.shape[0] // 2
+    sides = [pl.ds(0, half), pl.ds(half, half)]
+    curved_in_copy = [
+        pltpu.make_async_copy(curved_in.at[chunk], curved_ref.at[chunk], load_sem.at[chunk])
+        for chunk in range(chunks)
+    ]
+    flip_copy = [
+        pltpu.make_async_copy(flip_in.at[side], flip_ref.at[side], load_sem.at[chunks + place])
+        for place, side in enumerate(sides)
+    ]
+    cot_copy = pltpu.make_async_copy(cot_in, cot_ref, load_sem.at[chunks + 2])
+    for copy in [curved_in_copy[0], *flip_copy, *curved_in_copy[1:], cot_copy]:
+        copy.start()
+    stores = []
+
+    def store(source, target):
+        copy = pltpu.make_async_copy(source, target, store_sem.at[len(stores)])
+        copy.start()
+        stores.append(copy)
+
+    for chunk in range(chunks):
+        curved_in_copy[chunk].wait()
+        lanes = pl.ds(chunk * slim, slim)
+        for place, side in enumerate(sides):
+            if chunk == 0:
+                flip_copy[place].wait()
+            both = jnp.dot(
+                flip_ref[side, :], curved_ref[chunk, :, 0 : 2 * slim], preferred_element_type=jnp.float32
+            )
+            gate_ref[side, lanes] = both[:, 0:slim]
+            up_ref[side, lanes] = both[:, slim : 2 * slim]
+            store(gate_ref.at[side, lanes], gate_out.at[side, lanes])
+            store(up_ref.at[side, lanes], up_out.at[side, lanes])
+    cot_copy.wait()
+    for chunk in range(chunks):
+        lanes = pl.ds(chunk * slim, slim)
+        down_ref[lanes, :] = lax.dot_general(
+            curved_ref[chunk, :, 2 * slim : 3 * slim],
+            cot_ref[...],
+            (((0,), (0,)), ((), ())),
+            preferred_element_type=jnp.float32,
+        )
+        store(down_ref.at[lanes, :], down_out.at[lanes, :])
+    for copy in stores:
+        copy.wait()
 
 
 def local(
@@ -404,8 +484,11 @@
             jax.ShapeDtypeStruct((chunks, rows, 3 * slim), bf16),
         ),
         in_specs=[SPACE] * 4 + [HBM] * 6,
-        out_specs=(SPACE,) * 3,
+        out_specs=(HBM,) * 3,
         scratch_shapes=[
+            pltpu.VMEM((depth, rows), bf16),
+            pltpu.VMEM((rows, depth), bf16),
+            pltpu.VMEM((chunks, rows, 3 * slim), bf16),
             pltpu.VMEM((2, 4, 2, 2, BLOCK, width // 4), bf16),
             pltpu.VMEM((experts * BLOCK, 4 * count), bf16),
             pltpu.VMEM((2, 4 * count, width // 4), bf16),
@@ -424,7 +507,8 @@
         + [pltpu.SemaphoreType.DMA((parts * 2,))] * 2
         + [pltpu.SemaphoreType.DMA((parts * 4,))] * 4
         + [pltpu.SemaphoreType.DMA((chunks, 6))]
-        + [pltpu.SemaphoreType.DMA((units,))] * 8,
+        + [pltpu.SemaphoreType.DMA((units,))] * 8
+        + [pltpu.SemaphoreType.DMA((units + 2,))],
         compiler_params=pltpu.CompilerParams(
             collective_id=0, has_side_effects=True, vmem_limit_bytes=VMEM_LIMIT
         ),
@@ -433,26 +517,26 @@
         gate_proj[0], up_proj[0], gate_dir[0], up_dir[0], down_proj[0], down_dir[0],
     )
 
-    whole = lambda chunk: (0, 0)
     hess_gate, hess_up, hess_down = pl.pallas_call(
         product_kernel,
         name="products",
-        grid=(chunks,),
         out_shape=(
             jax.ShapeDtypeStruct((depth, hidden), f32),
             jax.ShapeDtypeStruct((depth, hidden), f32),
             jax.ShapeDtypeStruct((hidden, depth), f32),
         ),
-        in_specs=[
-            pl.BlockSpec((depth, rows), whole),
-            pl.BlockSpec((rows, depth), whole),
-            pl.BlockSpec((1, rows, 3 * slim), lambda chunk: (chunk, 0, 0)),
+        in_specs=[HBM] * 3,
+        out_specs=(HBM,) * 3,
+        scratch_shapes=[
+            pltpu.VMEM((depth, rows), bf16),
+            pltpu.VMEM((rows, depth), bf16),
+            pltpu.VMEM((chunks, rows, 3 * slim), bf16),
+            pltpu.VMEM((depth, hidden), f32),
+            pltpu.VMEM((depth, hidden), f32),
+            pltpu.VMEM((hidden, depth), f32),
+            pltpu.SemaphoreType.DMA((chunks + 3,)),
+            pltpu.SemaphoreType.DMA((5 * chunks,)),
         ],
-        out_specs=(
-            pl.BlockSpec((depth, slim), lambda chunk: (0, chunk)),
-            pl.BlockSpec((depth, slim), lambda chunk: (0, chunk)),
-            pl.BlockSpec((slim, depth), lambda chunk: (chunk, 0)),
-        ),
         compiler_params=pltpu.CompilerParams(vmem_limit_bytes=VMEM_LIMIT),
     )(flipped, cot, curved)
     return (hess_gate[None], hess_up[None], hess_down[None])

time: 125 us -> 114 us (0.912); the launches traced: 125 us -> 112 us
  Pallas kernels: 124 us -> 111 us
    pallas_call x1, Pallas kernels: 116 us -> 104 us  [local(): pl.pallas_call(layer_kernel, name='layer', out_shape=(jax.ShapeDtypeStruc...]
where the time goes in v5:
time: 114 us; the launch traced here: 112 us
  Pallas kernels  111 us (97%)
    pallas_call x1, Pallas kernels, local(): pl.pallas_call(layer_kernel, name='layer', out_shape=(jax.ShapeDtypeStruc...  104 us
    pallas_call x1, Pallas kernels, local(): pl.pallas_call(product_kernel, name='products', out_shape=(jax.ShapeDtype...  7.17 us

profile of v5, /device:TPU:1, one launch (start us, length us, event | category | flops | bytes accessed | tf_op | source)
XLA Modules:
  0.0 112.1 jit_solution(9529254659786780001)
XLA Ops:
  0.6 104.3 %layer.1 = (bf16[1024,768]{1,0:T(8,128)(2,1)}, bf16[768,1024]{1,0:T(8,128)(2,1)}, bf16[3,768,768]{2,1,0:T(8,128)(2,1)}) custom-call(bf16[128,2048]{1,0:T(8,128)(2,1)} %mine_ref.1, bf16[128,2048]{1,0:T(8,128)(2,1)} %cotan_ref.1, s32[1,128]{1,0:T(1,128)} %bitcast.17, f32[1,128]{1,0:T(1,128)} %bitcast.18, bf16[1024,768]{1,0:T(8,128)(2,1)} %bitcast.11, ...), custom_call_target="tpu_custom_call" | custom-call | tf_op jit(solution)/shard_map/layer/pallas_call | solution.py:478
  104.9 7.2 %products.1 = (f32[1024,768]{1,0:T(8,128)}, f32[1024,768]{1,0:T(8,128)}, f32[768,1024]{1,0:T(8,128)}) custom-call(bf16[1024,768]{1,0:T(8,128)(2,1)} %get-tuple-element.9.flip_in, bf16[768,1024]{1,0:T(8,128)(2,1)} %get-tuple-element.10.cot_in, bf16[3,768,768]{2,1,0:T(8,128)(2,1)} %get-tuple-element.11.curved_in), custom_call_target="tpu_custom_call" | custom-call | tf_op jit(solution)/shard_map/products/pallas_call | solution.py:520

commit v6 on v5

--- a/solution.py
+++ b/solution.py
@@ -16,9 +16,9 @@
 def layer_kernel(
     mine_ref, cotan_ref, route_ref, weight_ref, gate_ref, up_ref, gdir_ref, udir_ref, down_ref, ddir_ref,
     flip_out, cot_out, curved_out,
-    flip_ref, cot_ref, curved_ref, send_ref, pick_ref, feed_ref, first_ref, second_ref, packed_ref, tok_ref,
+    flip_ref, cot_ref, curved_ref, send_ref, pick_ref, feed_ref, early_ref, first_ref, second_ref, packed_ref, tok_ref,
     fwd_ref, bwd_ref, part_ref, core_in, chip_keep, chip_out, chip_in,
-    z_send, z_recv, x_send, x_recv, y_send, y_recv,
+    z_send, z_recv, x_send, x_recv, y_send, y_recv, early_y_send, early_y_recv, early_x_send, early_x_recv,
     load_sem, core_send, core_recv, chip_send, chip_recv, back_send, back_recv, last_send, last_recv, out_sem,
 ):
     tokens, width = mine_ref.shape
@@ -153,6 +153,44 @@
             y_send.at[part * 4 + to_y], y_recv.at[part * 4 + origin], plane(z, to_y),
         )
 
+    def early_y(to_low, to_high):
+        to_y = to_high * 2 + to_low
+        return transfer(
+            to_y == y, send_ref.at[:, z, :, to_low], early_ref.at[y],
+            early_y_send.at[to_y], early_y_recv.at[y], plane(z, to_y),
+        )
+
+    def early_x(turn, pair, to_core):
+        from_y = (y + turn) % 4
+        origin = (from_y % 2) * 2 + core
+        to_x = pair * 2 + from_y // 2
+        return transfer(
+            jnp.logical_and(to_x == x, to_core == core),
+            early_ref.at[from_y, to_core, pair],
+            packed_ref.at[origin, pl.ds(pl.multiple_of(x * BLOCK, BLOCK), BLOCK), :],
+            early_x_send.at[turn * 4 + pair * 2 + to_core], early_x_recv.at[origin * 4 + x], beside(to_x, to_core),
+        )
+
+    def hop_early():
+        for to_low in range(2):
+            for to_high in range(2):
+                early_y(to_low, to_high)[0]()
+
+    def pass_early():
+        for turn in (0, 1, 3, 2):
+            from_y = (y + turn) % 4
+            landed(early_ref.at[from_y], early_y_recv.at[from_y])
+            for pair in range(2):
+                for to_core in range(2):
+                    early_x(turn, pair, to_core)[0]()
+
+    def arrive_early():
+        for origin in range(4):
+            for number in range(4):
+                landed(
+                    packed_ref.at[origin, pl.ds(number * BLOCK, BLOCK), :], early_x_recv.at[origin * 4 + number]
+                )
+
     def hop_z(part, carry):
         for to_core in range(2):
             along_z(part, to_core)[0]()
@@ -176,7 +214,9 @@
         for number in range(4):
             landed(packed_ref.at[part * 4 + number], y_recv.at[part * 4 + number])
 
-    lax.fori_loop(0, 2, hop_z, 0)
+    hop_early()
+    hop_z(1, 0)
+    hop_z(2, 0)
     for chunk in range(chunks):
         for copy in loads(chunk):
             copy.start()
@@ -298,20 +338,11 @@
         back(unit, chip).start()
         return carry
 
-    def cross(step, carry):
-        hop_x(step)
-
-        @pl.when(step + 2 < parts)
-        def _():
-            hop_z(step + 2, 0)
-
-        @pl.when(step == 1)
-        def _():
-            hop_y(0)
-
-        return carry
-
-    lax.fori_loop(0, parts, cross, 0)
+    pass_early()
+    hop_z(3, 0)
+    hop_x(1)
+    hop_x(2)
+    hop_x(3)
 
     rows_out = [
         pltpu.make_async_copy(flip_ref, flip_out, out_sem.at[units]),
@@ -324,11 +355,16 @@
         return pltpu.make_async_copy(curved_ref.at[chunk, at, :], curved_out.at[chunk, at, :], out_sem.at[unit])
 
     def advance(step, carry):
-        @pl.when(step < parts)
+        @pl.when(step == 0)
+        def _():
+            arrive_early()
+            hop_y(1)
+
+        @pl.when(jnp.logical_and(step >= 1, step < parts))
         def _():
             arrive(step)
 
-        @pl.when(step + 1 < parts)
+        @pl.when(jnp.logical_and(step >= 1, step + 1 < parts))
         def _():
             hop_y(step + 1)
 
@@ -378,7 +414,12 @@
                 along_y(part, first, second)[1]()
         return carry
 
-    lax.fori_loop(0, parts, sent, 0)
+    lax.fori_loop(1, parts, sent, 0)
+    for first in range(2):
+        for second in range(2):
+            early_y(first, second)[1]()
+            for turn in range(4):
+                early_x(turn, first, second)[1]()
 
     def written(unit, carry):
         curved_copy(unit).wait()
@@ -492,6 +533,7 @@
             pltpu.VMEM((2, 4, 2, 2, BLOCK, width // 4), bf16),
             pltpu.VMEM((experts * BLOCK, 4 * count), bf16),
             pltpu.VMEM((2, 4 * count, width // 4), bf16),
+            pltpu.VMEM((4, 2, 2, BLOCK, width // 4), bf16),
             pltpu.VMEM((parts, 2, 2, 2, BLOCK, width // 4), bf16),
             pltpu.VMEM((parts, 2, 4 * BLOCK, width // 4), bf16),
             pltpu.VMEM((parts * 4, 4 * BLOCK, width // 4), bf16),
@@ -506,6 +548,8 @@
         ]
         + [pltpu.SemaphoreType.DMA((parts * 2,))] * 2
         + [pltpu.SemaphoreType.DMA((parts * 4,))] * 4
+        + [pltpu.SemaphoreType.DMA((4,))] * 2
+        + [pltpu.SemaphoreType.DMA((16,))] * 2
         + [pltpu.SemaphoreType.DMA((chunks, 6))]
         + [pltpu.SemaphoreType.DMA((units,))] * 8
         + [pltpu.SemaphoreType.DMA((units + 2,))],

time: 114 us -> 112 us (0.982)
    pallas_call x1, Pallas kernels: 104 us -> 103 us  [local(): pl.pallas_call(layer_kernel, name='layer', out_shape=(jax.ShapeDtypeStruc...]
where the time goes in v6:
time: 112 us; the launch traced here: 111 us
  Pallas kernels  110 us (98%)
    pallas_call x1, Pallas kernels, local(): pl.pallas_call(layer_kernel, name='layer', out_shape=(jax.ShapeDtypeStruc...  103 us
    pallas_call x1, Pallas kernels, local(): pl.pallas_call(product_kernel, name='products', out_shape=(jax.ShapeDtype...  7.17 us

profile of v6, /device:TPU:1, one launch (start us, length us, event | category | flops | bytes accessed | tf_op | source)
XLA Modules:
  0.0 110.7 jit_solution(7982069318684424893)
XLA Ops:
  0.6 102.9 %layer.1 = (bf16[1024,768]{1,0:T(8,128)(2,1)}, bf16[768,1024]{1,0:T(8,128)(2,1)}, bf16[3,768,768]{2,1,0:T(8,128)(2,1)}) custom-call(bf16[128,2048]{1,0:T(8,128)(2,1)} %mine_ref.1, bf16[128,2048]{1,0:T(8,128)(2,1)} %cotan_ref.1, s32[1,128]{1,0:T(1,128)} %bitcast.17, f32[1,128]{1,0:T(1,128)} %bitcast.18, bf16[1024,768]{1,0:T(8,128)(2,1)} %bitcast.11, ...), custom_call_target="tpu_custom_call" | custom-call | tf_op jit(solution)/shard_map/layer/pallas_call | solution.py:519
  103.6 7.2 %products.1 = (f32[1024,768]{1,0:T(8,128)}, f32[1024,768]{1,0:T(8,128)}, f32[768,1024]{1,0:T(8,128)}) custom-call(bf16[1024,768]{1,0:T(8,128)(2,1)} %get-tuple-element.9.flip_in, bf16[768,1024]{1,0:T(8,128)(2,1)} %get-tuple-element.10.cot_in, bf16[3,768,768]{2,1,0:T(8,128)(2,1)} %get-tuple-element.11.curved_in), custom_call_target="tpu_custom_call" | custom-call | tf_op jit(solution)/shard_map/products/pallas_call | solution.py:564

commit v7 on v6

--- a/solution.py
+++ b/solution.py
@@ -199,8 +199,7 @@
     def hop_x(part):
         for to_core in range(2):
             landed(first_ref.at[part, to_core], z_recv.at[part * 2 + to_core])
-        for pair in range(2):
-            for to_core in range(2):
+            for pair in range(2):
                 along_x(part, pair, to_core)[0]()
 
     def hop_y(part):
@@ -374,17 +373,17 @@
             for copy in rows_out:
                 copy.start()
 
-        @pl.when(step >= 2)
-        def _():
-            lax.fori_loop((step - 2) * chunks, (step - 2) * chunks + chunks, curve, 0)
-
         @pl.when(step < parts)
         def _():
             partial_products(step)
 
-        return carry
-
-    lax.fori_loop(0, parts + 2, advance, 0)
+        @pl.when(step >= 1)
+        def _():
+            lax.fori_loop((step - 1) * chunks, (step - 1) * chunks + chunks, curve, 0)
+
+        return carry
+
+    lax.fori_loop(0, parts + 1, advance, 0)
     def spread(unit, carry):
         back(unit, 1 - chip).wait_recv()
         last(unit, core).start()

time: 112 us -> 112 us (level)
  no operation moved by 1% of the time
where the time goes in v7:
time: 112 us; the launch traced here: 111 us
  Pallas kernels  110 us (98%)
    pallas_call x1, Pallas kernels, local(): pl.pallas_call(layer_kernel, name='layer', out_shape=(jax.ShapeDtypeStruc...  103 us
    pallas_call x1, Pallas kernels, local(): pl.pallas_call(product_kernel, name='products', out_shape=(jax.ShapeDtype...  7.17 us

profile of v7, /device:TPU:1, one launch (start us, length us, event | category | flops | bytes accessed | tf_op | source)
XLA Modules:
  0.0 110.7 jit_solution(5631405841409081281)
XLA Ops:
  0.6 102.9 %layer.1 = (bf16[1024,768]{1,0:T(8,128)(2,1)}, bf16[768,1024]{1,0:T(8,128)(2,1)}, bf16[3,768,768]{2,1,0:T(8,128)(2,1)}) custom-call(bf16[128,2048]{1,0:T(8,128)(2,1)} %mine_ref.1, bf16[128,2048]{1,0:T(8,128)(2,1)} %cotan_ref.1, s32[1,128]{1,0:T(1,128)} %bitcast.17, f32[1,128]{1,0:T(1,128)} %bitcast.18, bf16[1024,768]{1,0:T(8,128)(2,1)} %bitcast.11, ...), custom_call_target="tpu_custom_call" | custom-call | tf_op jit(solution)/shard_map/layer/pallas_call | solution.py:518
  103.5 7.2 %products.1 = (f32[1024,768]{1,0:T(8,128)}, f32[1024,768]{1,0:T(8,128)}, f32[768,1024]{1,0:T(8,128)}) custom-call(bf16[1024,768]{1,0:T(8,128)(2,1)} %get-tuple-element.9.flip_in, bf16[768,1024]{1,0:T(8,128)(2,1)} %get-tuple-element.10.cot_in, bf16[3,768,768]{2,1,0:T(8,128)(2,1)} %get-tuple-element.11.curved_in), custom_call_target="tpu_custom_call" | custom-call | tf_op jit(solution)/shard_map/products/pallas_call | solution.py:563
